TPU v7x, 768 devices: a whole 4x8x12 slice. The times are simulated.
768 devices in a mesh: fsdp: 24 (over z_hi, x, core), table: 32 (over y, z_lo).
Axes of the slice: x: 4, y: 8, z: 12 (z_hi: 3, z_lo: 4; z = z_hi * 4 + z_lo), core: 2. Of those that a mesh axis runs over, the one named last changes fastest.
Arguments:
- looked_up: bfloat16 [1536, 512, 192], P('fsdp', 'table'), may hold values from -6 to 6
- assignment: int32 [512], replicated, may hold values from 0 to 511, each once
- flat_weights: bfloat16 [1044480], P('fsdp'), as said below
- cotangent: bfloat16 [1536, 256, 192], P(('fsdp', 'table')), may hold values from -6 to 6
Outputs:
- layer_out: bfloat16 [1536, 256, 192], P(('fsdp', 'table'))
- emb_grad: bfloat16 [1536, 512, 192], P('fsdp', 'table')
- weight_grad: float32 [1044480], P('fsdp')
Inputs may be any that keep to these rules, and one draw needn't show every extreme that they name: `assignment`: every feature number appears exactly once. `flat_weights`: normal entries, each of the four weights scaled by its fan-in to the power -1/2 (512 for the first two, 4096 and 128 for the others).
All inputs are finite; a program needn't handle non-finite values.
Results may differ from a plain program's by a relative error of at most 0.0054.
Values may be sent and summed in bfloat16 or wider, within the bound.
A program may use at most 32 MiB of HBM per device.

v0:
```python
import jax
import jax.numpy as jnp
from jax import lax
from jax.sharding import PartitionSpec as P

NF = 512
D = 192
RANK = 8
HID = 128
NFM = 16
NLC = 240


def ln_rows(value_entries):
    average = jnp.mean(value_entries, axis=-1, keepdims=True)
    centred = value_entries - average
    spread = jnp.mean(centred * centred, axis=-1, keepdims=True)
    inverse_std = lax.rsqrt(spread + 1e-05)
    return (centred * inverse_std, inverse_std)


def split_weights(whole_weights):
    lin_end = NLC * NF
    proj_end = lin_end + NF * RANK
    up_end = proj_end + NF * RANK * HID
    linear_weight_matrix = whole_weights[:lin_end].reshape(NLC, NF)
    proj_weight = whole_weights[lin_end:proj_end].reshape(NF, RANK)
    up_weight = whole_weights[proj_end:up_end].reshape(NF * RANK, HID)
    out_weight = whole_weights[up_end:].reshape(HID, NFM * D)
    return (linear_weight_matrix, proj_weight, up_weight, out_weight)


def layer_pass(input_rows, cotangent, linear_weight_matrix, proj_weight, up_weight, out_weight):
    samples = input_rows.shape[0]
    single_float = jnp.float32
    compressed = jnp.einsum(
        "snd,nk->sdk", input_rows, proj_weight, preferred_element_type=single_float
    ).astype(jnp.bfloat16)
    pairwise = jnp.einsum(
        "snd,sdk->snk", input_rows, compressed, preferred_element_type=single_float
    )
    normed_full, pair_scale = ln_rows(pairwise.reshape(samples, NF * RANK))
    normed = normed_full.astype(jnp.bfloat16)
    preact = jnp.dot(normed, up_weight, preferred_element_type=single_float)
    hidden = jax.nn.silu(preact).astype(jnp.bfloat16)
    mixed = jnp.dot(hidden, out_weight, preferred_element_type=single_float).reshape(
        samples, NFM, D
    )
    linear_output = jnp.einsum(
        "rg,pgm->prm", linear_weight_matrix, input_rows, preferred_element_type=single_float
    )
    joined = jnp.concatenate([mixed, linear_output], axis=1)
    out_normed, out_scale = ln_rows(joined)
    result = out_normed.astype(jnp.bfloat16)
    upstream = cotangent.astype(single_float)
    d_joined = out_scale * (
        upstream
        - jnp.mean(upstream, axis=-1, keepdims=True)
        - out_normed * jnp.mean(upstream * out_normed, axis=-1, keepdims=True)
    )
    d_low = d_joined.astype(jnp.bfloat16)
    d_mixed = d_low[:, :NFM].reshape(samples, NFM * D)
    linear_branch_gradient = d_low[:, NFM:]
    grad_out = jnp.dot(hidden.T, d_mixed, preferred_element_type=single_float)
    d_hidden = jnp.dot(d_mixed, out_weight.T, preferred_element_type=single_float)
    logistic = jax.nn.sigmoid(preact)
    d_preact = (d_hidden * logistic * (1.0 + preact * (1.0 - logistic))).astype(jnp.bfloat16)
    grad_up = jnp.dot(normed.T, d_preact, preferred_element_type=single_float)
    d_normed = jnp.dot(d_preact, up_weight.T, preferred_element_type=single_float)
    d_flat = pair_scale * (
        d_normed
        - jnp.mean(d_normed, axis=-1, keepdims=True)
        - normed_full * jnp.mean(d_normed * normed_full, axis=-1, keepdims=True)
    )
    d_pairwise = d_flat.reshape(samples, NF, RANK).astype(jnp.bfloat16)
    from_pairs = jnp.einsum(
        "snk,sdk->snd", d_pairwise, compressed, preferred_element_type=single_float
    )
    d_compressed = jnp.einsum(
        "snd,snk->sdk", input_rows, d_pairwise, preferred_element_type=single_float
    ).astype(jnp.bfloat16)
    from_proj = jnp.einsum(
        "sdk,nk->snd", d_compressed, proj_weight, preferred_element_type=single_float
    )
    grad_proj = jnp.einsum(
        "snd,sdk->nk", input_rows, d_compressed, preferred_element_type=single_float
    )
    linear_weight_gradient = jnp.einsum(
        "ayi,axi->yx", linear_branch_gradient, input_rows, preferred_element_type=single_float
    )
    linear_branch_result = jnp.einsum(
        "uj,cuy->cjy",
        linear_weight_matrix,
        linear_branch_gradient,
        preferred_element_type=single_float,
    )
    d_input = (from_pairs + from_proj + linear_branch_result).astype(jnp.bfloat16)
    gradients = jnp.concatenate(
        [
            linear_weight_gradient.reshape(-1),
            grad_proj.reshape(-1),
            grad_up.reshape(-1),
            grad_out.reshape(-1),
        ]
    )
    return (result, d_input, gradients)


def shards(looked_up, assignment, flat_weights, cotangent):
    whole_weights = lax.all_gather(flat_weights, "fsdp", axis=0, tiled=True)
    arrived = lax.all_to_all(looked_up, "table", split_axis=0, concat_axis=1, tiled=True)
    inverse = jnp.argsort(assignment)
    ordered = jnp.take(arrived, inverse, axis=1)
    linear_weight_matrix, proj_weight, up_weight, out_weight = split_weights(whole_weights)
    result, d_input, gradients = layer_pass(
        ordered, cotangent, linear_weight_matrix, proj_weight, up_weight, out_weight
    )
    returned = jnp.take(d_input, assignment, axis=1)
    emb_grad = lax.all_to_all(returned, "table", split_axis=1, concat_axis=0, tiled=True)
    sample_total = arrived.shape[0] * lax.axis_size("fsdp") * lax.axis_size("table")
    partial_sums = lax.psum_scatter(gradients, "fsdp", scatter_dimension=0, tiled=True)
    summed = lax.psum(partial_sums, "table")
    weight_grad = summed / jnp.float32(sample_total)
    return (result, emb_grad, weight_grad)


def solution(mesh):
    return jax.shard_map(
        shards,
        mesh=mesh,
        in_specs=(P("fsdp", "table", None), P(), P("fsdp"), P(("fsdp", "table"), None, None)),
        out_specs=(P(("fsdp", "table"), None, None), P("fsdp", "table", None), P("fsdp")),
        check_vma=False,
    )
```

profile of v0, /device:TPU:6, one launch (start us, length us, event | category | flops | bytes accessed | tf_op | source)
XLA Modules:
  0.0 788.3 jit_solution(18279129404081219727)
XLA Ops:
  7.2 1.6 reshape.138
  8.9 12.9 %all-to-all-start = ((bf16[64,16,192]{2,1,0:T(8,128)(2,1)}), bf16[64,16,192]{2,1,0:T(8,128)(2,1)S(1)}, u32[]{:S(2)}, u32[]{:S(2)}) async-start(bf16[64,16,192]{2,1,0:T(8,128)(2,1)} %param.6), calls=%async_computation | async-start | bytes 1048576 | tf_op jit(solution)/shard_map/all_to_all | solution.py:111
  21.9 4.4 sort.17
  26.4 12.7 %all-to-all-done = bf16[64,16,192]{2,1,0:T(8,128)(2,1)S(1)} async-done(((bf16[64,16,192]{2,1,0:T(8,128)(2,1)}), bf16[64,16,192]{2,1,0:T(8,128)(2,1)S(1)}, u32[]{:S(2)}, u32[]{:S(2)}) %all-to-all-start) | async-done | bytes 393248 | tf_op jit(solution)/shard_map/all_to_all | solution.py:111
  39.1 0.5 copy.51
  39.6 2.6 gather_fusion
  42.2 1.8 fusion.7
  44.0 0.4 copy.54
  44.4 66.7 %all-gather.3.cloned.1.call-done = bf16[24,1,43520]{2,1,0:T(2,128)(2,1)} async-done(((bf16[1,1,43520]{2,1,0:T(2,128)(2,1)}), bf16[24,1,43520]{2,1,0:T(2,128)(2,1)}) %all-gather.3.cloned.1.call-update) | async-done | bytes 2088976 | tf_op jit(solution)/shard_map/all_gather | solution.py:110
  111.1 12.6 %reduce.2 = bf16[24,43520]{1,0:T(8,128)(2,1)S(1)} reduce(bf16[24,1,43520]{2,1,0:T(2,128)(2,1)} %all-gather.3.cloned.1.call-done, bf16[]{:T(256)} %constant.41), dimensions={1}, to_apply=%all-gather.reduce_sub_computation | reduce | bytes 4177922 | tf_op jit(solution)/shard_map/all_gather | solution.py:110
  123.7 4.5 reshape.139
  128.2 0.9 slice-done
  129.4 0.3 slice.63
  129.8 0.4 copy.56
  130.3 0.3 convolution_bitcast_fusion.5
  130.6 0.2 convolution_convert_fusion.1
  130.8 0.3 fusion.24
  131.3 0.3 reshape.114
  131.8 1.5 fusion.6
  133.3 0.5 fusion.20
  134.4 0.2 convert_reduce_fusion
  134.6 0.9 fusion.11
  135.7 0.3 fusion.4
  136.0 1.6 convolution_bitcast_fusion.1
  137.6 1.8 fusion.23
  139.4 0.6 convolution_bitcast_fusion
  140.0 1.2 convolution_bitcast_fusion.4
  141.3 0.3 convert_element_type.41
  141.7 0.2 convolution_convert_fusion
  141.9 2.9 copy.79
  144.7 1.0 convolution_bitcast_fusion.6
  145.8 1.1 reshape.117
  146.9 1.2 copy.78
  148.0 3.6 pad_maximum_fusion
  151.7 0.7 copy-done.1
  152.3 0.3 fusion.25
  152.7 0.3 fusion.1
  153.0 0.3 fusion.2
  153.3 0.4 copy.64
  153.7 2.6 gather_fusion.1
  156.3 2.5 fusion.8
  158.8 14.6 %all-to-all-start.1 = ((bf16[2,512,192]{2,0,1:T(2,128)(2,1)}), bf16[2,512,192]{2,0,1:T(2,128)(2,1)S(1)}, u32[]{:S(2)}, u32[]{:S(2)}) async-start(bf16[2,512,192]{2,0,1:T(2,128)(2,1)} %fusion.8), calls=%async_computation.1 | async-start | bytes 1048576 | tf_op jit(solution)/shard_map/all_to_all | solution.py:119
  173.5 1.3 dynamic-slice
  175.4 296.4 %all-reduce.6.cloned.1.call-done = f32[1044480]{0:T(1024)} async-done(((f32[1044480]{0:T(1024)}), f32[1044480]{0:T(1024)}) %all-reduce.6.cloned.1.call-update) | async-done | bytes 4177936
  471.8 1.7 dynamic-slice.1
  473.6 0.9 copy.66
  474.5 305.7 %all-reduce.4.cloned.1.call-done = f32[43520]{0:T(1024)} async-done(((f32[43520]{0:T(1024)}), f32[43520]{0:T(1024)}) %all-reduce.4.cloned.1.call-update) | async-done | bytes 174096 | tf_op jit(solution)/shard_map/psum | solution.py:122
  780.2 1.6 broadcast_multiply_fusion
  (42 shorter events, 2.0 us)
Async XLA Ops:
  7.2 103.9 %all-gather.3.cloned.1.call-start = ((), (), s32[]{:S(2)}) async-start(), calls=%async_computation.3 | async-start | bytes 4352000 | tf_op jit(solution)/shard_map/all_gather | solution.py:110
  8.9 30.1 %all-to-all-start = ((bf16[64,16,192]{2,1,0:T(8,128)(2,1)}), bf16[64,16,192]{2,1,0:T(8,128)(2,1)S(1)}, u32[]{:S(2)}, u32[]{:S(2)}) async-start(bf16[64,16,192]{2,1,0:T(8,128)(2,1)} %param.6), calls=%async_computation | async-start | bytes 1048576 | tf_op jit(solution)/shard_map/all_to_all | solution.py:111
  21.8 450.0 %all-reduce.6.cloned.1.call-start = ((), (), s32[]{:S(2)}) async-start(), calls=%async_computation.4 | async-start | bytes 8355840
  128.2 0.9 slice-start
  128.2 1.3 slice-start.1
  128.2 2.0 slice-start.2
  131.3 3.1 copy-start
  151.6 0.7 copy-start.1
  158.8 314.7 %all-to-all-start.1 = ((bf16[2,512,192]{2,0,1:T(2,128)(2,1)}), bf16[2,512,192]{2,0,1:T(2,128)(2,1)S(1)}, u32[]{:S(2)}, u32[]{:S(2)}) async-start(bf16[2,512,192]{2,0,1:T(2,128)(2,1)} %fusion.8), calls=%async_computation.1 | async-start | bytes 1048576 | tf_op jit(solution)/shard_map/all_to_all | solution.py:119
  173.4 606.8 %all-reduce.4.cloned.1.call-start = ((), (), s32[]{:S(2)}) async-start(), calls=%async_computation.2 | async-start | bytes 352256 | tf_op jit(solution)/shard_map/psum | solution.py:122
Sparse Core Ops, SparseCore 0:
  12.5 98.5 all-gather.2
  151.8 319.9 all-reduce.5
  475.6 304.5 all-reduce.3
where the time goes:
time: 790 us; the launch traced here: 788 us
  waiting for transfers between devices  682 us (86%)
  other arithmetic  28.3 us (4%)
  starting transfers between devices  27.6 us (3%)
  local copies, waits for them, and re-layouts  25.7 us (3%)
  between operations  14.7 us (2%)
  matrix products  10.5 us (1%)
    psum x1, waiting for transfers between devices, shards(): summed = lax.psum(partial_sums, 'table')  306 us
    unnamed x4, waiting for transfers between devices  296 us
    all_gather x1, waiting for transfers between devices, shards(): whole_weights = lax.all_gather(flat_weights, 'fsdp', axis=0, tiled=True)  66.7 us
  transfers between devices with their start and end apart: 5, of which 4 were waited for; matrix products, arithmetic and copies ran while one was open for 3% of the time, Pallas kernels for 0%

commit v1 on v0

v1 whole, which is shorter than its diff:
```python
import functools

import jax
import jax.numpy as jnp
import numpy as np
from jax import lax
from jax.experimental import pallas as pl
from jax.experimental.pallas import tpu as pltpu
from jax.sharding import PartitionSpec as P

NF = 512
D = 192
RANK = 8
HID = 128
NFM = 16
NLC = 240
NT = 32
NFS = 24
SHARD_ROWS = 340
PIECE_ROWS = 352
HALF_ROWS = PIECE_ROWS // 2
PROJ_ROW = 960
UP_ROW = 992
OUT_ROW = 5088
TOTAL_ROWS = 8160
SAMPLES = 1536.0
SLOTS = 16
MESH = pl.DeviceIdType.MESH
f32 = jnp.float32
bf16 = jnp.bfloat16


def _tables():
    owned = [[] for _ in range(NT)]
    for t in range(NT):
        for m in range(16):
            for k in range(8):
                owned[t].append((UP_ROW + 8 * (32 * m + t) + k, m * 8 + k))
        if t < 24:
            for h in range(HID):
                owned[t].append((OUT_ROW + 24 * h + t, 128 + h))
        for q in range(4):
            for m in range(8):
                if 32 * m + t < NLC:
                    owned[t].append((4 * (32 * m + t) + q, 256 + q * 8 + m))
        if t >= 3:
            owned[t].append((PROJ_ROW + t - 3, 288))
        if 3 <= t <= 5:
            owned[t].append((PROJ_ROW + 26 + t, 289))
    to_block = np.full((NT, 384), -1, np.int32)
    to_row = np.full((NFS, NT * SLOTS), -1, np.int32)
    seen = 0
    for t in range(NT):
        filled = [0] * NFS
        for row, place in sorted(owned[t]):
            f = row // SHARD_ROWS
            slot = filled[f]
            filled[f] += 1
            assert slot < SLOTS
            to_block[t, place] = f * SLOTS + slot
            to_row[f, t * SLOTS + slot] = row - f * SHARD_ROWS
            seen += 1
    assert seen == TOTAL_ROWS
    return to_block, to_row


TO_BLOCK, TO_ROW = _tables()


def iota(shape, dim):
    return lax.broadcasted_iota(jnp.int32, shape, dim)


def one_hot(condition):
    return jnp.where(condition, 1.0, 0.0).astype(bf16)


def nn(a, b):
    return lax.dot_general(a, b, (((1,), (0,)), ((), ())), preferred_element_type=f32)


def nt(a, b):
    return lax.dot_general(a, b, (((1,), (1,)), ((), ())), preferred_element_type=f32)


def tn(a, b):
    return lax.dot_general(a, b, (((0,), (0,)), ((), ())), preferred_element_type=f32)


def lanes(x, start, size):
    return lax.slice_in_dim(x, start, start + size, axis=1)


def rows(x, start, size):
    return lax.slice_in_dim(x, start, start + size, axis=0)


def arrive_kernel(lk_ref, w_ref, arr_ref, all_ref, pack, a_send, a_recv, w_send, w_recv, own_sem):
    t = lax.axis_index("table")
    f = lax.axis_index("fsdp")
    z, x, c = f // 8, (f // 2) % 4, f % 2

    def fs(zz, xx, cc):
        return ((z + zz) % 3) * 8 + ((x + xx) % 4) * 2 + (c + cc) % 2

    barrier = pltpu.get_barrier_semaphore()

    def greet(s, carry):
        pl.semaphore_signal(barrier, inc=1, device_id={"table": (t + s) % NT}, device_id_type=MESH)
        return carry

    near = (fs(1, 0, 0), fs(2, 0, 0), fs(0, 1, 0), fs(0, 3, 0), fs(0, 0, 1))
    for other in near:
        pl.semaphore_signal(barrier, inc=1, device_id={"fsdp": other}, device_id_type=MESH)
    lax.fori_loop(1, NT, greet, 0)

    pack[:, :, 0:D] = lk_ref[:, 0]
    pack[:, :, D : 2 * D] = lk_ref[:, 1]
    pl.semaphore_wait(barrier, NT - 1 + len(near))

    def piece(src, shard, index, to, part=None):
        dst = all_ref.at[shard]
        if part is not None:
            src = src.at[pl.ds(part * HALF_ROWS, HALF_ROWS)]
            dst = dst.at[pl.ds(part * HALF_ROWS, HALF_ROWS)]
        return pltpu.make_async_remote_copy(
            src_ref=src,
            dst_ref=dst,
            send_sem=w_send.at[index],
            recv_sem=w_recv.at[index],
            device_id={"fsdp": to},
            device_id_type=MESH,
        )

    sent = []

    def send(*args):
        copy = piece(*args)
        copy.start()
        sent.append(copy)

    def forward(shard, index, to, part=None):
        send(all_ref.at[shard], shard, index, to, part)

    def arrived(shard, index, part=None):
        piece(all_ref.at[shard], shard, index, f, part).wait_recv()

    up, down, right, left, sibling = near
    send(w_ref, f, 0, up)
    send(w_ref, f, 1, down)
    send(w_ref, f, 2, right)
    send(w_ref, f, 5, left)
    send(w_ref, f, 14, sibling)
    own = pltpu.make_async_copy(w_ref, all_ref.at[f], own_sem.at[0])
    own.start()
    mine = pltpu.make_async_copy(pack.at[t], arr_ref.at[t], own_sem.at[1])
    mine.start()

    def row_copy(s):
        to = (t + s) % NT
        return pltpu.make_async_remote_copy(
            src_ref=pack.at[to],
            dst_ref=arr_ref.at[t],
            send_sem=a_send.at[s],
            recv_sem=a_recv.at[s],
            device_id={"table": to},
            device_id_type=MESH,
        )

    def start_rows(s, carry):
        row_copy(s).start()
        return carry

    lax.fori_loop(1, NT, start_rows, 0)

    for index, dz in ((0, 2), (1, 1)):
        shard = fs(dz, 0, 0)
        arrived(shard, index)
        forward(shard, 2 + dz, right)
        forward(shard, 5 + dz, left)
        forward(shard, 14 + dz, sibling)
    for dz in (0, 2, 1):
        shard = fs(dz, 3, 0)
        arrived(shard, 2 + dz)
        forward(shard, 8 + dz, right, 0)
        forward(shard, 17 + dz, sibling)
        shard = fs(dz, 1, 0)
        arrived(shard, 5 + dz)
        forward(shard, 11 + dz, left, 1)
        forward(shard, 20 + dz, sibling)
    for dz in (0, 2, 1):
        shard = fs(dz, 2, 0)
        arrived(shard, 8 + dz, 0)
        forward(shard, 23 + dz, sibling, 0)
        arrived(shard, 11 + dz, 1)
        forward(shard, 26 + dz, sibling, 1)
    for dz in (0, 2, 1):
        arrived(fs(dz, 0, 1), 14 + dz)
        arrived(fs(dz, 3, 1), 17 + dz)
        arrived(fs(dz, 1, 1), 20 + dz)
        arrived(fs(dz, 2, 1), 23 + dz, 0)
        arrived(fs(dz, 2, 1), 26 + dz, 1)

    def wait_rows(s, carry):
        row_copy(s).wait_recv()
        return carry

    lax.fori_loop(1, NT, wait_rows, 0)
    own.wait()
    mine.wait()
    for copy in sent:
        copy.wait_send()

    def wait_sent(s, carry):
        row_copy(s).wait_send()
        return carry

    lax.fori_loop(1, NT, wait_sent, 0)


def spread(values, row_mod):
    lane = iota((16, 128), 1)
    keep = lane % 8 == row_mod
    out = []
    for v in range(32):
        source = lanes(values, 128 * (v // 8), 128)
        taken = jnp.take_along_axis(source, 16 * (v % 8) + lane // 8, axis=1)
        out.append(jnp.where(keep, taken, 0.0))
    return out


def gather_back(wide, row_mod):
    lane = iota((16, 128), 1)
    index = 8 * (lane % 16) + row_mod
    out = []
    for u in range(4):
        total = jnp.zeros((16, 128), f32)
        for w in range(8):
            taken = jnp.take_along_axis(lanes(wide, 128 * (8 * u + w), 128), index, axis=1)
            total = jnp.where(lane // 16 == w, taken, total)
        out.append(total)
    return jnp.concatenate(out, axis=1)


def layer_kernel(arr_ref, all_ref, as_row_ref, as_col_ref, cot_ref, out_ref, back_ref, msg_ref, nat, wout, msg):
    for f in range(NFS):
        nat[pl.ds(SHARD_ROWS * f, SHARD_ROWS), :] = all_ref[f].astype(f32)[:SHARD_ROWS]
    lin = jnp.concatenate([nat[pl.ds(q, NLC, stride=4), :] for q in range(4)], axis=1)
    lin = jnp.concatenate([lin, jnp.zeros((16, NF), f32)], axis=0).astype(bf16)
    for chunk in range(24):
        wout[:, 128 * chunk : 128 * chunk + 128] = nat[pl.ds(OUT_ROW + chunk, HID, stride=24), :].astype(bf16)
    proj_rows = nat[PROJ_ROW : PROJ_ROW + 32, :].astype(bf16)
    up = nat[UP_ROW : UP_ROW + NF * RANK, :].astype(bf16)

    r8 = one_hot(iota((8, 128), 1) % 8 == iota((8, 128), 0))
    flat_mask = iota((NF, 128), 1) // 8 == iota((NF, 128), 0) % 16
    picked = nn(one_hot(iota((NF, 32), 1) == iota((NF, 32), 0) // 16), proj_rows)
    picked = jnp.where(flat_mask, picked, 0.0).astype(bf16)
    proj_t = nt(r8, picked).astype(bf16)

    arrived = arr_ref[...]
    by_model = one_hot(as_row_ref[...] == iota((NF, NF), 0))
    by_table = one_hot(as_col_ref[...] == iota((NF, NF), 1))
    x = nn(by_model, arrived).astype(bf16)
    eye = one_hot(iota((2 * D, 2 * D), 0) == iota((2 * D, 2 * D), 1))
    xt = nt(eye, x).astype(bf16)

    half = iota((16, 2 * D), 1) // D == iota((16, 2 * D), 0) // 8
    comp = nn(proj_t, x)
    comp = jnp.concatenate([comp, comp], axis=0)
    comp = jnp.where(half, comp, 0.0).astype(bf16)
    pair = nt(comp, x)

    def per_sample(v):
        total = jnp.sum(v.reshape(2, 8, NF), axis=(1, 2), keepdims=True) * (1.0 / (NF * RANK))
        return jnp.broadcast_to(total, (2, 8, NF)).reshape(16, NF)

    centred = pair - per_sample(pair)
    pair_scale = lax.rsqrt(per_sample(centred * centred) + 1e-05)
    normed_full = centred * pair_scale
    normed = normed_full.astype(bf16)
    row_mod = iota((16, 128), 0) % 8
    wide = jnp.concatenate(spread(normed.astype(f32), row_mod), axis=1).astype(bf16)
    preact = jnp.sum(nn(wide, up).reshape(2, 8, HID), axis=1)
    logistic = 1.0 / (1.0 + jnp.exp(-preact))
    hidden = (preact / (1.0 + jnp.exp(-preact))).astype(bf16)
    mixed = nn(hidden, wout[...])

    def by_pairs(b):
        return jnp.concatenate([lanes(mixed[b : b + 1], 384 * e, 384) for e in range(8)], axis=0)

    m0, m1 = by_pairs(0), by_pairs(1)
    mix = jnp.concatenate(
        [
            jnp.concatenate([lanes(m0, 0, D), lanes(m1, 0, D)], axis=1),
            jnp.concatenate([lanes(m0, D, D), lanes(m1, D, D)], axis=1),
        ],
        axis=0,
    )
    mix = jnp.concatenate([jnp.zeros((112, 2 * D), f32), mix], axis=0).T
    linear = nt(xt, lin)
    joined = jnp.concatenate([lanes(linear, 0, 128), lanes(linear, 128, 128) + mix], axis=1)

    lane = iota((256, 256), 1)
    here = jnp.where(lane < NLC, lane + NFM, 2 * ((lane - NLC) % 8) + (lane - NLC) // 8)
    order = one_hot(here == iota((256, 256), 0))
    upstream = nn(cot_ref[...], order).reshape(2, D, 256)

    joined = joined.reshape(2, D, 256)
    mean = lambda v: jnp.mean(v, axis=1, keepdims=True)
    centred_out = joined - mean(joined)
    out_scale = lax.rsqrt(mean(centred_out * centred_out) + 1e-05)
    out_normed = centred_out * out_scale
    out_ref[...] = nt(out_normed.reshape(2 * D, 256).astype(bf16), order).astype(bf16)
    d_low = out_scale * (upstream - mean(upstream) - out_normed * mean(upstream * out_normed))
    d_low = d_low.reshape(2 * D, 256).astype(bf16)

    at = iota((272, 256), 0)
    wanted = 32 * (at % 8) + at // 8
    wanted = jnp.where(at >= 256, at - 256 + NLC, jnp.where(wanted < NLC, wanted, -1))
    d_rows = nt(one_hot(wanted == iota((272, 256), 1)), d_low)
    d_mix = rows(d_rows, 256, 16)
    grad_lin = nt(rows(d_rows, 0, 256).astype(bf16), x)
    d_pairs = [
        jnp.concatenate([lanes(d_mix[0:8], b * D, D), lanes(d_mix[8:16], b * D, D)], axis=1) for b in range(2)
    ]
    d_mixed = jnp.concatenate(
        [jnp.concatenate([d_pairs[b][e : e + 1] for e in range(8)], axis=1) for b in range(2)], axis=0
    )
    d_hidden = nt(d_mixed.astype(bf16), wout[...])
    d_preact = (d_hidden * logistic * (1.0 + preact * (1.0 - logistic))).astype(bf16)

    copies = jnp.concatenate(
        [jnp.broadcast_to(d_preact.astype(f32)[b : b + 1], (8, HID)) for b in range(2)], axis=0
    ).astype(bf16)
    d_normed = gather_back(nt(copies, up), row_mod)
    d_pair = pair_scale * (d_normed - per_sample(d_normed) - normed_full * per_sample(d_normed * normed_full))
    d_pair = d_pair.astype(bf16)

    d_comp = jnp.where(half, nn(d_pair, x), 0.0)
    d_comp = (d_comp[0:8] + d_comp[8:16]).astype(bf16)
    left = jnp.concatenate([comp, d_comp.astype(f32).astype(bf16)], axis=0)
    right = jnp.concatenate([d_pair, proj_t], axis=0)
    d_input = (tn(left, right) + nn(d_low, lin)).astype(bf16)
    back_ref[...] = nt(by_table, d_input).astype(bf16).reshape(NT, 16, 2 * D)

    grad_proj = nt(d_comp, x).astype(bf16)
    flat = jnp.where(flat_mask, tn(grad_proj, r8), 0.0).astype(bf16)
    at = iota((64, NF), 0)
    wanted = jnp.where(
        at < 32, jnp.where(at >= 3, at - 3, -1), jnp.where((at >= 35) & (at <= 37), at - 6, -1)
    )
    proj_out = nn(one_hot(wanted == iota((64, NF), 1) // 16), flat)
    p_lane = iota((NF, NF), 1)
    to_owner = one_hot(iota((NF, NF), 0) == (p_lane % 16) * 32 + p_lane // 16)
    by_owner = spread(nn(normed, to_owner), row_mod)
    msg[:, :, 256:384] = jnp.zeros((NT, 16, 128), f32)
    msg[:, 0:8, 0:256] = lanes(grad_lin, 0, 256).reshape(NT, 8, 256)
    msg[:, 8:16, 0:256] = lanes(grad_lin, 256, 256).reshape(NT, 8, 256)
    msg[:, 2:4, 256:384] = jnp.broadcast_to(hidden.astype(f32)[None], (NT, 2, HID))
    msg[:, 8:10, 256:384] = jnp.broadcast_to(d_preact.astype(f32)[None], (NT, 2, HID))
    for t in range(NT):
        msg[t, 0:2, 256:384] = jnp.sum(by_owner[t].reshape(2, 8, 128), axis=1)
        msg[t, 4:5, 256:384] = proj_out[t : t + 1]
        msg[t, 5:6, 256:384] = proj_out[32 + t : 33 + t]
        if t < 24:
            msg[t, 10:12, 256:384] = lanes(d_mixed, 128 * t, 128)
    msg_ref[...] = msg[...].astype(bf16)


def leave_kernel(
    back_ref, msg_ref, block_ref, row_ref, emb_ref, grad_ref,
    rec, got, blocks, parts, mine, whole, b_send, b_recv, m_send, m_recv, f_send, f_recv, g_send, g_recv,
):
    t = lax.axis_index("table")
    f = lax.axis_index("fsdp")

    barrier = pltpu.get_barrier_semaphore()

    def greet_table(s, carry):
        pl.semaphore_signal(barrier, inc=1, device_id={"table": (t + s) % NT}, device_id_type=MESH)
        return carry

    def greet_fsdp(s, carry):
        pl.semaphore_signal(barrier, inc=1, device_id={"fsdp": (f + s) % NFS}, device_id_type=MESH)
        return carry

    lax.fori_loop(1, NT, greet_table, 0)
    lax.fori_loop(1, NFS, greet_fsdp, 0)
    pl.semaphore_wait(barrier, NT - 1 + NFS - 1)

    def to_table(s, src, dst, send_sem, recv_sem):
        to = (t + s) % NT
        return pltpu.make_async_remote_copy(
            src_ref=src if src is mine else src.at[to],
            dst_ref=dst.at[t],
            send_sem=send_sem.at[s],
            recv_sem=recv_sem.at[s],
            device_id={"table": to},
            device_id_type=MESH,
        )

    def to_fsdp(s):
        to = (f + s) % NFS
        return pltpu.make_async_remote_copy(
            src_ref=blocks.at[to],
            dst_ref=parts.at[f],
            send_sem=f_send.at[s],
            recv_sem=f_recv.at[s],
            device_id={"fsdp": to},
            device_id_type=MESH,
        )

    def each(n, act):
        def step(s, carry):
            act(s)
            return carry

        lax.fori_loop(1, n, step, 0)

    msg_copy = lambda s: to_table(s, msg_ref, got, m_send, m_recv)
    row_copy = lambda s: to_table(s, back_ref, rec, b_send, b_recv)
    all_copy = lambda s: to_table(s, mine, whole, g_send, g_recv)

    each(NT, lambda s: msg_copy(s).start())
    each(NT, lambda s: row_copy(s).start())
    got[pl.ds(t, 1)] = msg_ref[pl.ds(t, 1)]
    rec[pl.ds(t, 1)] = back_ref[pl.ds(t, 1)]
    place = one_hot(iota((NFS * SLOTS, 384), 0) == block_ref[pl.ds(t, 1), :])
    final = one_hot(iota((PIECE_ROWS, NT * SLOTS), 0) == row_ref[pl.ds(f, 1), :])

    each(NT, lambda s: msg_copy(s).wait_recv())
    linear = jnp.sum(got[:, :, 0:256].astype(f32), axis=0)
    factors = got[:, :, 256:384].astype(f32)
    first = factors[:, 0:8].reshape(NT * 8, 128)
    second = factors[:, 8:16].reshape(NT * 8, 128).astype(bf16)
    at = iota((NT * 8, 128), 0) % 8
    left = jnp.concatenate([jnp.where(at < 2, first, 0.0), jnp.where((at == 2) | (at == 3), first, 0.0)], axis=1)
    products = tn(left.astype(bf16), second)
    tail = jnp.sum(factors[:, 0:8], axis=0)[4:6]
    sums = jnp.concatenate(
        [
            products,
            linear[0:8, 0:128],
            linear[0:8, 128:256],
            linear[8:16, 0:128],
            linear[8:16, 128:256],
            tail,
            jnp.zeros((94, 128), f32),
        ],
        axis=0,
    ).astype(bf16)
    blocks[...] = nn(place, sums).astype(bf16).reshape(NFS, SLOTS, 128)

    each(NFS, lambda s: to_fsdp(s).start())
    parts[pl.ds(f, 1)] = blocks[pl.ds(f, 1)]
    each(NFS, lambda s: to_fsdp(s).wait_recv())
    mine[...] = jnp.sum(parts[...].astype(f32), axis=0).astype(bf16)

    each(NT, lambda s: all_copy(s).start())
    whole[pl.ds(t, 1)] = mine[...][None]
    each(NT, lambda s: all_copy(s).wait_recv())
    grad_ref[...] = nn(final, whole[...].reshape(NT * SLOTS, 128)) * (1.0 / SAMPLES)

    each(NT, lambda s: row_copy(s).wait_recv())
    emb_ref[:, 0] = rec[:, :, 0:D]
    emb_ref[:, 1] = rec[:, :, D : 2 * D]
    each(NT, lambda s: msg_copy(s).wait_send())
    each(NT, lambda s: row_copy(s).wait_send())
    each(NT, lambda s: all_copy(s).wait_send())
    each(NFS, lambda s: to_fsdp(s).wait_send())


VMEM = pl.BlockSpec(memory_space=pltpu.VMEM)
LIMIT = 56 * 1024 * 1024


def arrive(looked, shard):
    return pl.pallas_call(
        arrive_kernel,
        out_shape=(
            jax.ShapeDtypeStruct((NT, 16, 2 * D), bf16),
            jax.ShapeDtypeStruct((NFS, PIECE_ROWS, 128), bf16),
        ),
        in_specs=[VMEM] * 2,
        out_specs=(VMEM, VMEM),
        scratch_shapes=[
            pltpu.VMEM((NT, 16, 2 * D), bf16),
            pltpu.SemaphoreType.DMA((NT,)),
            pltpu.SemaphoreType.DMA((NT,)),
            pltpu.SemaphoreType.DMA((29,)),
            pltpu.SemaphoreType.DMA((29,)),
            pltpu.SemaphoreType.DMA((2,)),
        ],
        compiler_params=pltpu.CompilerParams(collective_id=0, has_side_effects=True, vmem_limit_bytes=LIMIT),
    )(looked, shard)


def layer(arrived, weights, as_row, as_col, cotangent):
    return pl.pallas_call(
        layer_kernel,
        out_shape=(
            jax.ShapeDtypeStruct((2 * D, 256), bf16),
            jax.ShapeDtypeStruct((NT, 16, 2 * D), bf16),
            jax.ShapeDtypeStruct((NT, 16, 2 * D), bf16),
        ),
        in_specs=[VMEM] * 5,
        out_specs=(VMEM, VMEM, VMEM),
        scratch_shapes=[
            pltpu.VMEM((TOTAL_ROWS, 128), f32),
            pltpu.VMEM((HID, NFM * D), bf16),
            pltpu.VMEM((NT, 16, 2 * D), f32),
        ],
        compiler_params=pltpu.CompilerParams(vmem_limit_bytes=LIMIT),
    )(arrived, weights, as_row, as_col, cotangent)


def leave(back, message):
    return pl.pallas_call(
        leave_kernel,
        out_shape=(
            jax.ShapeDtypeStruct((NT, 2, 16, D), bf16),
            jax.ShapeDtypeStruct((PIECE_ROWS, 128), f32),
        ),
        in_specs=[VMEM] * 4,
        out_specs=(VMEM, VMEM),
        scratch_shapes=[
            pltpu.VMEM((NT, 16, 2 * D), bf16),
            pltpu.VMEM((NT, 16, 2 * D), bf16),
            pltpu.VMEM((NFS, SLOTS, 128), bf16),
            pltpu.VMEM((NFS, SLOTS, 128), bf16),
            pltpu.VMEM((SLOTS, 128), bf16),
            pltpu.VMEM((NT, SLOTS, 128), bf16),
        ]
        + [pltpu.SemaphoreType.DMA((NT,))] * 8,
        compiler_params=pltpu.CompilerParams(collective_id=1, has_side_effects=True, vmem_limit_bytes=LIMIT),
    )(back, message, jnp.asarray(TO_BLOCK), jnp.asarray(TO_ROW))


def shards(looked_up, assignment, flat_weights, cotangent):
    shard = jnp.pad(flat_weights.reshape(SHARD_ROWS, 128), ((0, PIECE_ROWS - SHARD_ROWS), (0, 0)))
    arrived, weights = arrive(looked_up.reshape(NT, 2, 16, D), shard)
    out, back, message = layer(
        arrived.reshape(NF, 2 * D),
        weights,
        assignment.reshape(1, NF),
        assignment.reshape(NF, 1),
        cotangent.transpose(0, 2, 1).reshape(2 * D, 256),
    )
    emb, grad = leave(back, message)
    layer_out = out.reshape(2, D, 256).transpose(0, 2, 1)
    return layer_out, emb.reshape(2 * NT, 16, D), grad[:SHARD_ROWS].reshape(SHARD_ROWS * 128)


def solution(mesh):
    return jax.shard_map(
        shards,
        mesh=mesh,
        in_specs=(P("fsdp", "table", None), P(), P("fsdp"), P(("fsdp", "table"), None, None)),
        out_specs=(P(("fsdp", "table"), None, None), P("fsdp", "table", None), P("fsdp")),
        check_vma=False,
    )
```

time: 790 us -> 103 us (0.13)
  waiting for transfers between devices: 682 us -> 0 us
  Pallas kernels: 0 us -> 94.3 us
  other arithmetic: 28.3 us -> 0 us
  starting transfers between devices: 27.6 us -> 0 us
  local copies, waits for them, and re-layouts: 25.7 us -> 6.56 us
  between operations: 14.7 us -> 0.65 us
  matrix products: 10.5 us -> 0 us
    psum x1 -> x0, waiting for transfers between devices: 306 us -> none  [shards(): summed = lax.psum(partial_sums, 'table')]
    unnamed x4 -> x0, waiting for transfers between devices: 296 us -> none
    pallas_call x0 -> x3, Pallas kernels: none -> 94.3 us  [the longest x1 43.2 us: leave(): pl.pallas_call(leave_kernel, out_shape=(jax.ShapeDtypeStruct((NT, 2, 16,...]
    all_gather x1 -> x0, waiting for transfers between devices: 66.7 us -> none  [shards(): whole_weights = lax.all_gather(flat_weights, 'fsdp', axis=0, tiled=True)]
    all_to_all x2 -> x0, starting transfers between devices: 27.5 us -> none  [the longest x1 14.6 us: shards(): lax.all_to_all(returned, 'table', split_axis=1, concat_axis=0, tiled=True)]
    all_to_all x2 -> x0, waiting for transfers between devices: 12.7 us -> none  [the longest x1 12.7 us: shards(): lax.all_to_all(looked_up, 'table', split_axis=0, concat_axis=1, tiled=True)]
    all_gather x1 -> x0, other arithmetic: 12.6 us -> none  [shards(): whole_weights = lax.all_gather(flat_weights, 'fsdp', axis=0, tiled=True)]
    unnamed x10 -> x1, local copies, waits for them, and re-layouts: 13.8 us -> 1.87 us
  transfers between devices with their start and end apart: 5 -> 0, of which waited for: 4 -> 0; matrix products, arithmetic and copies ran while one was open for 3% -> 0% of each run, Pallas kernels for 0% -> 0%
where the time goes in v1:
time: 103 us; the launch traced here: 101 us
  Pallas kernels  94.3 us (92%)
  local copies, waits for them, and re-layouts  6.56 us (6%)
    pallas_call x1, Pallas kernels, leave(): pl.pallas_call(leave_kernel, out_shape=(jax.ShapeDtypeStruct((NT, 2, 16,...  43.2 us
    pallas_call x1, Pallas kernels, arrive(): pl.pallas_call(arrive_kernel, out_shape=(jax.ShapeDtypeStruct((NT, 16, 2...  43.1 us
    pallas_call x1, Pallas kernels, layer(): pl.pallas_call(layer_kernel, out_shape=(jax.ShapeDtypeStruct((2 * D, 256)...  8.05 us

profile of v1, /device:TPU:6, one launch (start us, length us, event | category | flops | bytes accessed | tf_op | source)
XLA Modules:
  0.0 101.5 jit_solution(3241025771611436328)
XLA Ops:
  0.6 1.5 %pad.4.w_ref = bf16[352,128]{1,0:T(8,128)(2,1)} pad(bf16[340,128]{1,0:T(8,128)(2,1)} %bitcast.18, bf16[]{:T(256)} %constant.6.clone.1), padding=0_12x0_0 | pad | bytes 177154 | tf_op jit(solution)/shard_map/jit(_pad)/pad | solution.py:541
  2.2 1.6 %copy.9.as_col_ref = s32[512,1]{1,0:T(8,128)} copy(s32[512,1]{0,1:T(1,128)} %bitcast.19) | data formatting | bytes 4096 | tf_op jit(solution)/shard_map/reshape | solution.py:547
  3.7 43.1 %shard_map.85 = (bf16[32,16,384]{2,1,0:T(8,128)(2,1)}, bf16[24,352,128]{2,1,0:T(8,128)(2,1)}) custom-call(bf16[32,2,16,192]{3,2,1,0:T(8,128)(2,1)} %bitcast.14, bf16[352,128]{1,0:T(8,128)(2,1)} %pad.4.w_ref), custom_call_target="tpu_custom_call" | custom-call | tf_op jit(solution)/shard_map/pallas_call | solution.py:479
  46.8 8.0 %shard_map.86 = (bf16[384,256]{1,0:T(8,128)(2,1)}, bf16[32,16,384]{2,1,0:T(8,128)(2,1)}, bf16[32,16,384]{2,1,0:T(8,128)(2,1)}) custom-call(bf16[512,384]{1,0:T(8,128)(2,1)} %bitcast.16, bf16[24,352,128]{2,1,0:T(8,128)(2,1)} %get-tuple-element.11.all_ref, s32[1,512]{1,0:T(1,128)} %bitcast.20, s32[512,1]{1,0:T(8,128)} %copy.9.as_col_ref, bf16[384,256]{1,0:T(8,128)(2,1)} %bitcast.17), custom_call_target="tpu_custom_call" | custom-call | tf_op jit(solution)/shard_map/pallas_call | solution.py:500
  54.8 43.2 %shard_map.87 = (bf16[32,2,16,192]{3,2,1,0:T(8,128)(2,1)}, f32[352,128]{1,0:T(8,128)}) custom-call(bf16[32,16,384]{2,1,0:T(8,128)(2,1)} %get-tuple-element.13.back_ref, bf16[32,16,384]{2,1,0:T(8,128)(2,1)} %get-tuple-element.14.msg_ref, s32[32,384]{1,0:T(8,128)} %constant.7.clone.block_ref, s32[24,512]{1,0:T(8,128)} %constant.8.clone.row_ref), custom_call_target="tpu_custom_call" | custom-call | tf_op jit(solution)/shard_map/pallas_call | solution.py:519
  98.0 1.6 %slice_bitcast_fusion = f32[43520]{0:T(1024)} fusion(f32[352,128]{1,0:T(8,128)} %get-tuple-element.16), kind=kLoop, calls=%fused_computation | loop fusion | bytes 348160 | tf_op jit(solution)/shard_map/reshape | solution.py:552
  99.6 1.9 %copy.11 = bf16[64,16,192]{2,1,0:T(8,128)(2,1)} copy(bf16[64,16,192]{2,1,0:T(8,128)(2,1)} %bitcast.15) | data formatting | bytes 786432

commit v2 on v1

v2 whole, which is shorter than its diff:
```python
import functools

import jax
import jax.numpy as jnp
import numpy as np
from jax import lax
from jax.experimental import pallas as pl
from jax.experimental.pallas import tpu as pltpu
from jax.sharding import PartitionSpec as P

NF = 512
D = 192
RANK = 8
HID = 128
NFM = 16
NLC = 240
NT = 32
NFS = 24
SHARD_ROWS = 340
PIECE_ROWS = 352
HALF_ROWS = PIECE_ROWS // 2
PROJ_ROW = 960
UP_ROW = 992
OUT_ROW = 5088
TOTAL_ROWS = 8160
SAMPLES = 1536.0
SLOTS = 16
MESH = pl.DeviceIdType.MESH
f32 = jnp.float32
bf16 = jnp.bfloat16


def _tables():
    owned = [[] for _ in range(NT)]
    for t in range(NT):
        for m in range(16):
            for k in range(8):
                owned[t].append((UP_ROW + 8 * (32 * m + t) + k, m * 8 + k))
        if t < 24:
            for h in range(HID):
                owned[t].append((OUT_ROW + 24 * h + t, 128 + h))
        for q in range(4):
            for m in range(8):
                if 32 * m + t < NLC:
                    owned[t].append((4 * (32 * m + t) + q, 256 + q * 8 + m))
        if t >= 3:
            owned[t].append((PROJ_ROW + t - 3, 288))
        if 3 <= t <= 5:
            owned[t].append((PROJ_ROW + 26 + t, 289))
    to_block = np.full((NT, 384), -1, np.int32)
    to_row = np.full((NFS, NT * SLOTS), -1, np.int32)
    seen = 0
    for t in range(NT):
        filled = [0] * NFS
        for row, place in sorted(owned[t]):
            f = row // SHARD_ROWS
            slot = filled[f]
            filled[f] += 1
            assert slot < SLOTS
            to_block[t, place] = f * SLOTS + slot
            to_row[f, t * SLOTS + slot] = row - f * SHARD_ROWS
            seen += 1
    assert seen == TOTAL_ROWS
    return to_block, to_row


TO_BLOCK, TO_ROW = _tables()


def iota(shape, dim):
    return lax.broadcasted_iota(jnp.int32, shape, dim)


def one_hot(condition):
    return jnp.where(condition, 1.0, 0.0).astype(bf16)


def nn(a, b):
    return lax.dot_general(a, b, (((1,), (0,)), ((), ())), preferred_element_type=f32)


def nt(a, b):
    return lax.dot_general(a, b, (((1,), (1,)), ((), ())), preferred_element_type=f32)


def tn(a, b):
    return lax.dot_general(a, b, (((0,), (0,)), ((), ())), preferred_element_type=f32)


def lanes(x, start, size):
    return lax.slice_in_dim(x, start, start + size, axis=1)


def rows(x, start, size):
    return lax.slice_in_dim(x, start, start + size, axis=0)


def spread(values, row_mod):
    lane = iota((16, 128), 1)
    keep = lane % 8 == row_mod
    out = []
    for v in range(32):
        source = lanes(values, 128 * (v // 8), 128)
        taken = jnp.take_along_axis(source, 16 * (v % 8) + lane // 8, axis=1)
        out.append(jnp.where(keep, taken, 0.0))
    return out


def gather_back(wide, row_mod):
    lane = iota((16, 128), 1)
    index = 8 * (lane % 16) + row_mod
    out = []
    for u in range(4):
        total = jnp.zeros((16, 128), f32)
        for w in range(8):
            taken = jnp.take_along_axis(lanes(wide, 128 * (8 * u + w), 128), index, axis=1)
            total = jnp.where(lane // 16 == w, taken, total)
        out.append(total)
    return jnp.concatenate(out, axis=1)


def whole_kernel(
    lk_ref, w_ref, as_row_ref, cot_ref, block_ref, out_ref, rec_ref, whole_ref,
    pack, padded, arr, all_ref, nat, wout, by_model, order, upstream, lin_msg, fac_msg, back, fac,
    got_lin, got_fac, blocks, parts, mine,
    own_sem, a_send, a_recv, w_send, w_recv, l_send, l_recv, m_send, m_recv, b_send, b_recv, f_send, f_recv, g_send, g_recv,
):
    t = lax.axis_index("table")
    f = lax.axis_index("fsdp")
    z, xx, c = f // 8, (f // 2) % 4, f % 2

    def fs(dz, dx, dc):
        return ((z + dz) % 3) * 8 + ((xx + dx) % 4) * 2 + (c + dc) % 2

    def each(n, act):
        def step(s, carry):
            act(s)
            return carry

        lax.fori_loop(1, n, step, 0)

    def to_table(src, dst, send_sem, recv_sem):
        def copy(s):
            to = (t + s) % NT
            return pltpu.make_async_remote_copy(
                src_ref=src if src is mine else src.at[to],
                dst_ref=dst.at[t],
                send_sem=send_sem.at[s],
                recv_sem=recv_sem.at[s],
                device_id={"table": to},
                device_id_type=MESH,
            )

        return copy

    def to_fsdp(s):
        to = (f + s) % NFS
        return pltpu.make_async_remote_copy(
            src_ref=blocks.at[to],
            dst_ref=parts.at[f],
            send_sem=f_send.at[s],
            recv_sem=f_recv.at[s],
            device_id={"fsdp": to},
            device_id_type=MESH,
        )

    row_in = to_table(pack, arr, a_send, a_recv)
    lin_out = to_table(lin_msg, got_lin, l_send, l_recv)
    fac_out = to_table(fac_msg, got_fac, m_send, m_recv)
    row_out = to_table(back, rec_ref, b_send, b_recv)
    all_out = to_table(mine, whole_ref, g_send, g_recv)

    barrier = pltpu.get_barrier_semaphore()
    near = (fs(1, 0, 0), fs(2, 0, 0), fs(0, 1, 0), fs(0, 3, 0), fs(0, 0, 1))
    each(NT, lambda s: pl.semaphore_signal(barrier, inc=1, device_id={"table": (t + s) % NT}, device_id_type=MESH))
    for other in near:
        pl.semaphore_signal(barrier, inc=1, device_id={"fsdp": other}, device_id_type=MESH)
    padded[0:SHARD_ROWS] = w_ref[...]
    padded[SHARD_ROWS:PIECE_ROWS] = jnp.zeros((PIECE_ROWS - SHARD_ROWS, 128), bf16)
    pack[:, :, 0:D] = lk_ref[:, 0]
    pack[:, :, D : 2 * D] = lk_ref[:, 1]
    pl.semaphore_wait(barrier, NT - 1 + len(near))

    def piece(src, shard, index, to, part=None):
        dst = all_ref.at[shard]
        if part is not None:
            src = src.at[pl.ds(part * HALF_ROWS, HALF_ROWS)]
            dst = dst.at[pl.ds(part * HALF_ROWS, HALF_ROWS)]
        return pltpu.make_async_remote_copy(
            src_ref=src,
            dst_ref=dst,
            send_sem=w_send.at[index],
            recv_sem=w_recv.at[index],
            device_id={"fsdp": to},
            device_id_type=MESH,
        )

    sent = []

    def send(*args):
        copy = piece(*args)
        copy.start()
        sent.append(copy)

    def forward(shard, index, to, part=None):
        send(all_ref.at[shard], shard, index, to, part)

    def arrived(shard, index, part=None):
        piece(all_ref.at[shard], shard, index, f, part).wait_recv()

    up_z, down_z, right, left, sibling = near
    send(padded, f, 0, up_z)
    send(padded, f, 1, down_z)
    send(padded, f, 2, right)
    send(padded, f, 5, left)
    send(padded, f, 14, sibling)
    each(NT, lambda s: row_in(s).start())
    all_ref[pl.ds(f, 1)] = padded[...][None]
    arr[pl.ds(t, 1)] = pack[pl.ds(t, 1)]

    by_model[...] = one_hot(as_row_ref[...] == iota((NF, NF), 0))
    lane = iota((256, 256), 1)
    here = jnp.where(lane < NLC, lane + NFM, 2 * ((lane - NLC) % 8) + (lane - NLC) // 8)
    order[...] = one_hot(here == iota((256, 256), 0))
    upstream[...] = nn(cot_ref[...], order[...])

    def turn(dz):
        shard = fs(dz, 3, 0)
        arrived(shard, 2 + dz)
        forward(shard, 8 + dz, right, 0)
        forward(shard, 17 + dz, sibling)
        shard = fs(dz, 1, 0)
        arrived(shard, 5 + dz)
        forward(shard, 11 + dz, left, 1)
        forward(shard, 20 + dz, sibling)

    def opposite(dz):
        shard = fs(dz, 2, 0)
        arrived(shard, 8 + dz, 0)
        forward(shard, 23 + dz, sibling, 0)
        arrived(shard, 11 + dz, 1)
        forward(shard, 26 + dz, sibling, 1)

    def assemble(dz, dx):
        column = ((z + dz) % 3) * 4 + (xx + dx) % 4
        both = [all_ref[2 * column + core].astype(f32)[:SHARD_ROWS] for core in range(2)]
        at = pl.multiple_of(2 * SHARD_ROWS * column, 8)
        nat[pl.ds(at, 2 * SHARD_ROWS), :] = jnp.concatenate(both, axis=0)

    def others(dz):
        arrived(fs(dz, 0, 1), 14 + dz)
        assemble(dz, 0)
        arrived(fs(dz, 3, 1), 17 + dz)
        assemble(dz, 3)
        arrived(fs(dz, 1, 1), 20 + dz)
        assemble(dz, 1)
        arrived(fs(dz, 2, 1), 23 + dz, 0)
        arrived(fs(dz, 2, 1), 26 + dz, 1)
        assemble(dz, 2)

    turn(0)
    for index, dz in ((0, 2), (1, 1)):
        shard = fs(dz, 0, 0)
        arrived(shard, index)
        forward(shard, 2 + dz, right)
        forward(shard, 5 + dz, left)
        forward(shard, 14 + dz, sibling)
    opposite(0)
    turn(2)
    turn(1)
    others(0)
    opposite(2)
    opposite(1)

    each(NT, lambda s: row_in(s).wait_recv())
    x = nn(by_model[...], arr[...].reshape(NF, 2 * D)).astype(bf16)
    eye = one_hot(iota((2 * D, 2 * D), 0) == iota((2 * D, 2 * D), 1))
    xt = nt(eye, x).astype(bf16)

    others(2)
    others(1)

    lin = jnp.concatenate([nat[pl.ds(q, NLC, stride=4), :] for q in range(4)], axis=1)
    lin = jnp.concatenate([lin, jnp.zeros((16, NF), f32)], axis=0).astype(bf16)
    for chunk in range(24):
        wout[:, 128 * chunk : 128 * chunk + 128] = nat[pl.ds(OUT_ROW + chunk, HID, stride=24), :].astype(bf16)
    proj_rows = nat[PROJ_ROW : PROJ_ROW + 32, :].astype(bf16)
    up = nat[UP_ROW : UP_ROW + NF * RANK, :].astype(bf16)

    r8 = one_hot(iota((8, 128), 1) % 8 == iota((8, 128), 0))
    flat_mask = iota((NF, 128), 1) // 8 == iota((NF, 128), 0) % 16
    picked = nn(one_hot(iota((NF, 32), 1) == iota((NF, 32), 0) // 16), proj_rows)
    picked = jnp.where(flat_mask, picked, 0.0).astype(bf16)
    proj_t = nt(r8, picked).astype(bf16)

    half = iota((16, 2 * D), 1) // D == iota((16, 2 * D), 0) // 8
    comp = nn(proj_t, x)
    comp = jnp.concatenate([comp, comp], axis=0)
    comp = jnp.where(half, comp, 0.0).astype(bf16)
    pair = nt(comp, x)

    def per_sample(v):
        total = jnp.sum(v.reshape(2, 8, NF), axis=(1, 2), keepdims=True) * (1.0 / (NF * RANK))
        return jnp.broadcast_to(total, (2, 8, NF)).reshape(16, NF)

    centred = pair - per_sample(pair)
    pair_scale = lax.rsqrt(per_sample(centred * centred) + 1e-05)
    normed_full = centred * pair_scale
    normed = normed_full.astype(bf16)
    row_mod = iota((16, 128), 0) % 8
    wide = jnp.concatenate(spread(normed.astype(f32), row_mod), axis=1).astype(bf16)
    preact = jnp.sum(nn(wide, up).reshape(2, 8, HID), axis=1)
    logistic = 1.0 / (1.0 + jnp.exp(-preact))
    hidden = (preact / (1.0 + jnp.exp(-preact))).astype(bf16)
    mixed = nn(hidden, wout[...])

    def by_pairs(b):
        return jnp.concatenate([lanes(mixed[b : b + 1], 384 * e, 384) for e in range(8)], axis=0)

    m0, m1 = by_pairs(0), by_pairs(1)
    mix = jnp.concatenate(
        [
            jnp.concatenate([lanes(m0, 0, D), lanes(m1, 0, D)], axis=1),
            jnp.concatenate([lanes(m0, D, D), lanes(m1, D, D)], axis=1),
        ],
        axis=0,
    )
    mix = jnp.concatenate([jnp.zeros((112, 2 * D), f32), mix], axis=0).T
    linear = nt(xt, lin)
    joined = jnp.concatenate([lanes(linear, 0, 128), lanes(linear, 128, 128) + mix], axis=1)

    joined = joined.reshape(2, D, 256)
    mean = lambda v: jnp.mean(v, axis=1, keepdims=True)
    centred_out = joined - mean(joined)
    out_scale = lax.rsqrt(mean(centred_out * centred_out) + 1e-05)
    out_normed = centred_out * out_scale
    cot = upstream[...].reshape(2, D, 256)
    d_low = out_scale * (cot - mean(cot) - out_normed * mean(cot * out_normed))
    d_low = d_low.reshape(2 * D, 256).astype(bf16)

    at = iota((272, 256), 0)
    wanted = 32 * (at % 8) + at // 8
    wanted = jnp.where(at >= 256, at - 256 + NLC, jnp.where(wanted < NLC, wanted, -1))
    d_rows = nt(one_hot(wanted == iota((272, 256), 1)), d_low)
    grad_lin = nt(rows(d_rows, 0, 256).astype(bf16), x)
    lin_msg[...] = jnp.concatenate(
        [lanes(grad_lin, 0, 256).reshape(NT, 8, 256), lanes(grad_lin, 256, 256).reshape(NT, 8, 256)], axis=1
    ).astype(bf16)
    each(NT, lambda s: lin_out(s).start())

    d_mix = rows(d_rows, 256, 16)
    d_pairs = [
        jnp.concatenate([lanes(d_mix[0:8], b * D, D), lanes(d_mix[8:16], b * D, D)], axis=1) for b in range(2)
    ]
    d_mixed = jnp.concatenate(
        [jnp.concatenate([d_pairs[b][e : e + 1] for e in range(8)], axis=1) for b in range(2)], axis=0
    )
    d_hidden = nt(d_mixed.astype(bf16), wout[...])
    d_preact = (d_hidden * logistic * (1.0 + preact * (1.0 - logistic))).astype(bf16)

    copies = jnp.concatenate(
        [jnp.broadcast_to(d_preact.astype(f32)[b : b + 1], (8, HID)) for b in range(2)], axis=0
    ).astype(bf16)
    d_normed = gather_back(nt(copies, up), row_mod)
    d_pair = pair_scale * (d_normed - per_sample(d_normed) - normed_full * per_sample(d_normed * normed_full))
    d_pair = d_pair.astype(bf16)

    d_comp = jnp.where(half, nn(d_pair, x), 0.0)
    d_comp = (d_comp[0:8] + d_comp[8:16]).astype(bf16)

    grad_proj = nt(d_comp, x).astype(bf16)
    flat = jnp.where(flat_mask, tn(grad_proj, r8), 0.0).astype(bf16)
    at = iota((64, NF), 0)
    wanted = jnp.where(
        at < 32, jnp.where(at >= 3, at - 3, -1), jnp.where((at >= 35) & (at <= 37), at - 6, -1)
    )
    proj_out = nn(one_hot(wanted == iota((64, NF), 1) // 16), flat)
    p_lane = iota((NF, NF), 1)
    to_owner = one_hot(iota((NF, NF), 0) == (p_lane % 16) * 32 + p_lane // 16)
    by_owner = spread(nn(normed, to_owner), row_mod)
    fac[...] = jnp.zeros((NT, 16, 128), f32)
    fac[:, 2:4] = jnp.broadcast_to(hidden.astype(f32)[None], (NT, 2, HID))
    fac[:, 8:10] = jnp.broadcast_to(d_preact.astype(f32)[None], (NT, 2, HID))
    for i in range(NT):
        fac[i, 0:2] = jnp.sum(by_owner[i].reshape(2, 8, 128), axis=1)
        fac[i, 4:5] = proj_out[i : i + 1]
        fac[i, 5:6] = proj_out[32 + i : 33 + i]
        if i < 24:
            fac[i, 10:12] = lanes(d_mixed, 128 * i, 128)
    fac_msg[...] = fac[...].astype(bf16)
    each(NT, lambda s: fac_out(s).start())

    left_side = jnp.concatenate([comp, d_comp], axis=0)
    right_side = jnp.concatenate([d_pair, proj_t], axis=0)
    d_input = (tn(left_side, right_side) + nn(d_low, lin)).astype(bf16)
    back[...] = lax.dot_general(
        by_model[...], d_input, (((0,), (1,)), ((), ())), preferred_element_type=f32
    ).astype(bf16).reshape(NT, 16, 2 * D)
    each(NT, lambda s: row_out(s).start())

    got_lin[pl.ds(t, 1)] = lin_msg[pl.ds(t, 1)]
    got_fac[pl.ds(t, 1)] = fac_msg[pl.ds(t, 1)]
    rec_ref[pl.ds(t, 1)] = back[pl.ds(t, 1)]
    out_ref[...] = nt(out_normed.reshape(2 * D, 256).astype(bf16), order[...]).astype(bf16)
    place = one_hot(iota((NFS * SLOTS, 384), 0) == block_ref[pl.ds(t, 1), :])

    each(NT, lambda s: lin_out(s).wait_recv())
    linear = jnp.sum(got_lin[...].astype(f32), axis=0)
    each(NT, lambda s: fac_out(s).wait_recv())
    factors = got_fac[...].astype(f32)
    first = factors[:, 0:8].reshape(NT * 8, 128)
    second = factors[:, 8:16].reshape(NT * 8, 128).astype(bf16)
    at = iota((NT * 8, 128), 0) % 8
    left_side = jnp.concatenate([jnp.where(at < 2, first, 0.0), jnp.where((at == 2) | (at == 3), first, 0.0)], axis=1)
    products = tn(left_side.astype(bf16), second)
    tail = jnp.sum(factors[:, 0:8], axis=0)[4:6]
    sums = jnp.concatenate(
        [
            products,
            linear[0:8, 0:128],
            linear[0:8, 128:256],
            linear[8:16, 0:128],
            linear[8:16, 128:256],
            tail,
            jnp.zeros((94, 128), f32),
        ],
        axis=0,
    ).astype(bf16)
    blocks[...] = nn(place, sums).astype(bf16).reshape(NFS, SLOTS, 128)

    each(NFS, lambda s: to_fsdp(s).start())
    parts[pl.ds(f, 1)] = blocks[pl.ds(f, 1)]
    each(NFS, lambda s: to_fsdp(s).wait_recv())
    mine[...] = jnp.sum(parts[...].astype(f32), axis=0).astype(bf16)

    each(NT, lambda s: all_out(s).start())
    whole_ref[pl.ds(t, 1)] = mine[...][None]
    each(NT, lambda s: all_out(s).wait_recv())
    each(NT, lambda s: row_out(s).wait_recv())

    for copy in sent:
        copy.wait_send()
    for copies in (row_in, lin_out, fac_out, row_out, all_out):
        each(NT, lambda s: copies(s).wait_send())
    each(NFS, lambda s: to_fsdp(s).wait_send())


def finish_kernel(out_ref, rec_ref, whole_ref, row_ref, layer_ref, emb_ref, grad_ref):
    f = lax.axis_index("fsdp")
    layer_ref[...] = out_ref[...]
    emb_ref[:, 0] = rec_ref[:, :, 0:D]
    emb_ref[:, 1] = rec_ref[:, :, D : 2 * D]
    final = one_hot(iota((SHARD_ROWS, NT * SLOTS), 0) == row_ref[pl.ds(f, 1), :])
    grad_ref[...] = nn(final, whole_ref[...].reshape(NT * SLOTS, 128)) * (1.0 / SAMPLES)


VMEM = pl.BlockSpec(memory_space=pltpu.VMEM)
LIMIT = 40 * 1024 * 1024


def shape(dtype, *size):
    return jax.ShapeDtypeStruct(size, dtype)


def whole(looked, shard, as_row, cotangent):
    return pl.pallas_call(
        whole_kernel,
        out_shape=(shape(bf16, 2 * D, 256), shape(bf16, NT, 16, 2 * D), shape(bf16, NT, SLOTS, 128)),
        in_specs=[VMEM] * 5,
        out_specs=(VMEM,) * 3,
        scratch_shapes=[
            pltpu.VMEM((NT, 16, 2 * D), bf16),
            pltpu.VMEM((PIECE_ROWS, 128), bf16),
            pltpu.VMEM((NT, 16, 2 * D), bf16),
            pltpu.VMEM((NFS, PIECE_ROWS, 128), bf16),
            pltpu.VMEM((TOTAL_ROWS, 128), f32),
            pltpu.VMEM((HID, NFM * D), bf16),
            pltpu.VMEM((NF, NF), bf16),
            pltpu.VMEM((256, 256), bf16),
            pltpu.VMEM((2 * D, 256), f32),
            pltpu.VMEM((NT, 16, 256), bf16),
            pltpu.VMEM((NT, 16, 128), bf16),
            pltpu.VMEM((NT, 16, 2 * D), bf16),
            pltpu.VMEM((NT, 16, 128), f32),
            pltpu.VMEM((NT, 16, 256), bf16),
            pltpu.VMEM((NT, 16, 128), bf16),
            pltpu.VMEM((NFS, SLOTS, 128), bf16),
            pltpu.VMEM((NFS, SLOTS, 128), bf16),
            pltpu.VMEM((SLOTS, 128), bf16),
            pltpu.SemaphoreType.DMA((2,)),
        ]
        + [pltpu.SemaphoreType.DMA((NT,))] * 14,
        compiler_params=pltpu.CompilerParams(collective_id=0, has_side_effects=True, vmem_limit_bytes=LIMIT),
    )(looked, shard, as_row, cotangent, jnp.asarray(TO_BLOCK))


def finish(out, rec, gathered):
    return pl.pallas_call(
        finish_kernel,
        out_shape=(shape(bf16, 2 * D, 256), shape(bf16, NT, 2, 16, D), shape(f32, SHARD_ROWS, 128)),
        in_specs=[VMEM] * 4,
        out_specs=(VMEM,) * 3,
    )(out, rec, gathered, jnp.asarray(TO_ROW))


def shards(looked_up, assignment, flat_weights, cotangent):
    out, rec, gathered = whole(
        looked_up.reshape(NT, 2, 16, D),
        flat_weights.reshape(SHARD_ROWS, 128),
        assignment.reshape(1, NF),
        cotangent.transpose(0, 2, 1).reshape(2 * D, 256),
    )
    layer_out, emb, grad = finish(out, rec, gathered)
    return layer_out.reshape(2, D, 256).transpose(0, 2, 1), emb.reshape(2 * NT, 16, D), grad.reshape(SHARD_ROWS * 128)


def solution(mesh):
    return jax.shard_map(
        shards,
        mesh=mesh,
        in_specs=(P("fsdp", "table", None), P(), P("fsdp"), P(("fsdp", "table"), None, None)),
        out_specs=(P(("fsdp", "table"), None, None), P("fsdp", "table", None), P("fsdp")),
        check_vma=False,
    )
```

time: 103 us -> 88.9 us (0.86)
  Pallas kernels: 94.3 us -> 80.9 us
    pallas_call x3 -> x2, Pallas kernels: 94.3 us -> 80.9 us  [the longest x1 78.7 us: whole(): pl.pallas_call(whole_kernel, out_shape=(shape(bf16, 2 * D, 256), shape(bf...]
    unnamed x1 -> x16, local copies, waits for them, and re-layouts: 1.87 us -> 6.37 us
    reshape x2 -> x0, local copies, waits for them, and re-layouts: 3.16 us -> none  [the longest x1 1.6 us: shards(): grad[:SHARD_ROWS].reshape(SHARD_ROWS * 128)]
    pad x1 -> x0, local copies, waits for them, and re-layouts: 1.54 us -> none  [shards(): jnp.pad(flat_weights.reshape(SHARD_ROWS, 128), ((0, PIECE_ROWS - SHARD_RO...]
where the time goes in v2:
time: 88.9 us; the launch traced here: 88 us
  Pallas kernels  80.9 us (91%)
  local copies, waits for them, and re-layouts  6.37 us (7%)
    pallas_call x1, Pallas kernels, whole(): pl.pallas_call(whole_kernel, out_shape=(shape(bf16, 2 * D, 256), shape(bf...  78.7 us
    unnamed x16, local copies, waits for them, and re-layouts  6.37 us
    pallas_call x1, Pallas kernels, finish(): pl.pallas_call(finish_kernel, out_shape=(shape(bf16, 2 * D, 256), shape(b...  2.23 us

profile of v2, /device:TPU:6, one launch (start us, length us, event | category | flops | bytes accessed | tf_op | source)
XLA Modules:
  0.0 88.0 jit_solution(16178630021902520944)
XLA Ops:
  0.6 0.0 copy-start.7
  0.6 0.7 copy-done.7
  1.3 0.0 copy-start
  1.3 1.0 %copy-done = bf16[64,16,192]{2,1,0:T(8,128)(2,1)S(1)} copy-done((bf16[64,16,192]{2,1,0:T(8,128)(2,1)S(1)}, bf16[64,16,192]{2,1,0:T(8,128)(2,1)}, u32[]{:S(2)}) %copy-start) | copy-done | bytes 393240
  2.4 0.0 copy-start.2
  2.4 0.9 %copy-done.2 = bf16[2,256,192]{1,2,0:T(8,128)(2,1)S(1)} copy-done((bf16[2,256,192]{1,2,0:T(8,128)(2,1)S(1)}, bf16[2,256,192]{1,2,0:T(8,128)(2,1)}, u32[]{:S(2)}) %copy-start.2) | copy-done | bytes 196632
  3.3 0.0 copy-start.5
  3.3 0.9 %copy-done.5 = bf16[43520]{0:T(1024)(128)(2,1)S(1)} copy-done((bf16[43520]{0:T(1024)(128)(2,1)S(1)}, bf16[43520]{0:T(1024)(128)(2,1)}, u32[]{:S(2)}) %copy-start.5) | copy-done | bytes 87064
  4.2 0.0 copy-start.6
  4.2 0.8 copy-done.6
  5.0 78.7 %shard_map.85 = (bf16[384,256]{1,0:T(8,128)(2,1)S(1)}, bf16[32,16,384]{2,1,0:T(8,128)(2,1)S(1)}, bf16[32,16,128]{2,1,0:T(8,128)(2,1)S(1)}) custom-call(bf16[32,2,16,192]{3,2,1,0:T(8,128)(2,1)S(1)} %bitcast.11, bf16[340,128]{1,0:T(8,128)(2,1)S(1)} %bitcast.13, s32[1,512]{1,0:T(1,128)S(1)} %bitcast.14, bf16[384,256]{1,0:T(8,128)(2,1)S(1)} %bitcast.12, ...), custom_call_target="tpu_custom_call" | custom-call | tf_op jit(solution)/shard_map/pallas_call | solution.py:466
  83.7 0.0 copy-start.1
  83.7 0.7 copy-done.1
  84.4 0.0 copy-start.3
  84.4 0.7 copy-done.3
  85.1 0.0 copy-start.4
  85.1 0.6 copy-done.4
  85.7 2.2 %shard_map.86 = (bf16[384,256]{1,0:T(8,128)(2,1)}, bf16[32,2,16,192]{3,2,1,0:T(8,128)(2,1)}, f32[340,128]{1,0:T(8,128)}) custom-call(bf16[384,256]{1,0:T(8,128)(2,1)} %copy-done.3, bf16[32,16,384]{2,1,0:T(8,128)(2,1)} %copy-done.1, bf16[32,16,128]{2,1,0:T(8,128)(2,1)} %copy-done.4, s32[24,512]{1,0:T(8,128)} %constant.5.clone.row_ref), custom_call_target="tpu_custom_call" | custom-call | tf_op jit(solution)/shard_map/pallas_call | solution.py:498
Async XLA Ops:
  0.6 0.7 copy-start.7
  1.3 1.0 %copy-start = (bf16[64,16,192]{2,1,0:T(8,128)(2,1)S(1)}, bf16[64,16,192]{2,1,0:T(8,128)(2,1)}, u32[]{:S(2)}) copy-start(bf16[64,16,192]{2,1,0:T(8,128)(2,1)} %param.6) | copy-start | bytes 1179652
  2.4 0.9 %copy-start.2 = (bf16[2,256,192]{1,2,0:T(8,128)(2,1)S(1)}, bf16[2,256,192]{1,2,0:T(8,128)(2,1)}, u32[]{:S(2)}) copy-start(bf16[2,256,192]{1,2,0:T(8,128)(2,1)} %param.9) | copy-start | bytes 589828
  3.3 0.9 %copy-start.5 = (bf16[43520]{0:T(1024)(128)(2,1)S(1)}, bf16[43520]{0:T(1024)(128)(2,1)}, u32[]{:S(2)}) copy-start(bf16[43520]{0:T(1024)(128)(2,1)} %param.8) | copy-start | bytes 261124
  4.2 0.8 copy-start.6
  83.7 0.7 copy-start.1
  84.4 0.7 copy-start.3
  85.1 0.6 copy-start.4

commit v3 on v2

--- a/solution.py
+++ b/solution.py
@@ -120,10 +120,10 @@
 
 
 def whole_kernel(
-    lk_ref, w_ref, as_row_ref, cot_ref, block_ref, out_ref, rec_ref, whole_ref,
-    pack, padded, arr, all_ref, nat, wout, by_model, order, upstream, lin_msg, fac_msg, back, fac,
+    lk_hbm, w_hbm, as_row_hbm, cot_hbm, block_hbm, out_hbm, rec_ref, whole_ref,
+    lk_ref, w_ref, as_row_ref, cot_ref, block_ref, out_ref, pack, padded, arr, all_ref, nat, wout, by_model, order, upstream, pair_out, pair_in, kept, lin_msg, fac_msg, back,
     got_lin, got_fac, blocks, parts, mine,
-    own_sem, a_send, a_recv, w_send, w_recv, l_send, l_recv, m_send, m_recv, b_send, b_recv, f_send, f_recv, g_send, g_recv,
+    own_sem, in_sem, w_send, w_recv, ex_send, ex_recv,
 ):
     t = lax.axis_index("table")
     f = lax.axis_index("fsdp")
@@ -139,56 +139,83 @@
 
         lax.fori_loop(1, n, step, 0)
 
-    def to_table(src, dst, send_sem, recv_sem):
-        def copy(s):
-            to = (t + s) % NT
-            return pltpu.make_async_remote_copy(
-                src_ref=src if src is mine else src.at[to],
-                dst_ref=dst.at[t],
-                send_sem=send_sem.at[s],
-                recv_sem=recv_sem.at[s],
-                device_id={"table": to},
+    class Exchange:
+        def __init__(self, axis, src, dst, index):
+            me, self.n = (t, NT) if axis == "table" else (f, NFS)
+
+            def copy(s):
+                to = (me + s) % self.n
+                return pltpu.make_async_remote_copy(
+                    src_ref=src if src is mine else src.at[to],
+                    dst_ref=dst.at[me],
+                    send_sem=ex_send.at[index],
+                    recv_sem=ex_recv.at[index],
+                    device_id={axis: to},
+                    device_id_type=MESH,
+                )
+
+            self.copy = copy
+            every = dst.at[pl.ds(0, self.n - 1)]
+            self.every = lambda: pltpu.make_async_remote_copy(
+                src_ref=every,
+                dst_ref=every,
+                send_sem=ex_send.at[index],
+                recv_sem=ex_recv.at[index],
+                device_id={axis: me},
                 device_id_type=MESH,
             )
 
-        return copy
-
-    def to_fsdp(s):
-        to = (f + s) % NFS
-        return pltpu.make_async_remote_copy(
-            src_ref=blocks.at[to],
-            dst_ref=parts.at[f],
-            send_sem=f_send.at[s],
-            recv_sem=f_recv.at[s],
-            device_id={"fsdp": to},
-            device_id_type=MESH,
-        )
-
-    row_in = to_table(pack, arr, a_send, a_recv)
-    lin_out = to_table(lin_msg, got_lin, l_send, l_recv)
-    fac_out = to_table(fac_msg, got_fac, m_send, m_recv)
-    row_out = to_table(back, rec_ref, b_send, b_recv)
-    all_out = to_table(mine, whole_ref, g_send, g_recv)
+        def start(self):
+            each(self.n, lambda s: self.copy(s).start())
+            started.append(self)
+
+        def wait(self):
+            self.every().wait_recv()
+            received.append(self)
+
+        def wait_send(self):
+            self.every().wait_send()
+
+    started = []
+    received = []
+    row_in = Exchange("table", pack, arr, 0)
+    lin_out = Exchange("table", lin_msg, got_lin, 1)
+    fac_out = Exchange("table", fac_msg, got_fac, 2)
+    row_out = Exchange("table", back, rec_ref, 3)
+    all_out = Exchange("table", mine, whole_ref, 4)
+    to_fsdp = Exchange("fsdp", blocks, parts, 5)
+
+    def local(src, dst, index):
+        return pltpu.make_async_copy(src, dst, in_sem.at[index])
+
+    inputs = [
+        local(w_hbm, w_ref, 0),
+        local(lk_hbm, lk_ref, 1),
+        local(as_row_hbm, as_row_ref, 2),
+        local(cot_hbm, cot_ref, 3),
+        local(block_hbm, block_ref, 4),
+    ]
+    for copy in inputs:
+        copy.start()
 
     barrier = pltpu.get_barrier_semaphore()
     near = (fs(1, 0, 0), fs(2, 0, 0), fs(0, 1, 0), fs(0, 3, 0), fs(0, 0, 1))
     each(NT, lambda s: pl.semaphore_signal(barrier, inc=1, device_id={"table": (t + s) % NT}, device_id_type=MESH))
     for other in near:
         pl.semaphore_signal(barrier, inc=1, device_id={"fsdp": other}, device_id_type=MESH)
+    inputs[0].wait()
     padded[0:SHARD_ROWS] = w_ref[...]
     padded[SHARD_ROWS:PIECE_ROWS] = jnp.zeros((PIECE_ROWS - SHARD_ROWS, 128), bf16)
+    inputs[1].wait()
     pack[:, :, 0:D] = lk_ref[:, 0]
     pack[:, :, D : 2 * D] = lk_ref[:, 1]
     pl.semaphore_wait(barrier, NT - 1 + len(near))
 
-    def piece(src, shard, index, to, part=None):
-        dst = all_ref.at[shard]
-        if part is not None:
-            src = src.at[pl.ds(part * HALF_ROWS, HALF_ROWS)]
-            dst = dst.at[pl.ds(part * HALF_ROWS, HALF_ROWS)]
+    def piece(src, shard, part, index, to):
+        at = pl.ds(part * HALF_ROWS, HALF_ROWS)
         return pltpu.make_async_remote_copy(
-            src_ref=src,
-            dst_ref=dst,
+            src_ref=src.at[at],
+            dst_ref=all_ref.at[shard, at],
             send_sem=w_send.at[index],
             recv_sem=w_recv.at[index],
             device_id={"fsdp": to},
@@ -196,50 +223,74 @@
         )
 
     sent = []
+    locals_started = []
+
+    def drain():
+        for copy in locals_started:
+            copy.wait()
+        for copy in sent:
+            copy.wait_send()
+        for exchange in started:
+            if exchange not in received:
+                exchange.wait()
+        for exchange in started:
+            exchange.wait_send()
 
     def send(*args):
         copy = piece(*args)
         copy.start()
         sent.append(copy)
 
-    def forward(shard, index, to, part=None):
-        send(all_ref.at[shard], shard, index, to, part)
-
-    def arrived(shard, index, part=None):
-        piece(all_ref.at[shard], shard, index, f, part).wait_recv()
+    def forward(shard, part, index, to):
+        send(all_ref.at[shard], shard, part, index + part, to)
+
+    def arrived(shard, part, index):
+        piece(all_ref.at[shard], shard, part, index + part, f).wait_recv()
 
     up_z, down_z, right, left, sibling = near
-    send(padded, f, 0, up_z)
-    send(padded, f, 1, down_z)
-    send(padded, f, 2, right)
-    send(padded, f, 5, left)
-    send(padded, f, 14, sibling)
-    each(NT, lambda s: row_in(s).start())
+    for part in range(2):
+        send(padded, f, part, part, up_z)
+        send(padded, f, part, 2 + part, down_z)
+    for part in range(2):
+        send(padded, f, part, 4 + part, right)
+        send(padded, f, part, 10 + part, left)
+        send(padded, f, part, 22 + part, sibling)
+    row_in.start()
     all_ref[pl.ds(f, 1)] = padded[...][None]
     arr[pl.ds(t, 1)] = pack[pl.ds(t, 1)]
 
+    for copy in inputs[2:]:
+        copy.wait()
     by_model[...] = one_hot(as_row_ref[...] == iota((NF, NF), 0))
     lane = iota((256, 256), 1)
     here = jnp.where(lane < NLC, lane + NFM, 2 * ((lane - NLC) % 8) + (lane - NLC) // 8)
     order[...] = one_hot(here == iota((256, 256), 0))
     upstream[...] = nn(cot_ref[...], order[...])
 
-    def turn(dz):
+    def from_z(part):
+        for index, dz in ((0, 2), (2, 1)):
+            shard = fs(dz, 0, 0)
+            arrived(shard, part, index)
+            forward(shard, part, 4 + 2 * dz, right)
+            forward(shard, part, 10 + 2 * dz, left)
+            forward(shard, part, 22 + 8 * dz, sibling)
+
+    def turn(dz, part):
         shard = fs(dz, 3, 0)
-        arrived(shard, 2 + dz)
-        forward(shard, 8 + dz, right, 0)
-        forward(shard, 17 + dz, sibling)
+        arrived(shard, part, 4 + 2 * dz)
+        if part == 0:
+            forward(shard, part, 16 + 2 * dz, right)
+        forward(shard, part, 22 + 8 * dz + 6, sibling)
         shard = fs(dz, 1, 0)
-        arrived(shard, 5 + dz)
-        forward(shard, 11 + dz, left, 1)
-        forward(shard, 20 + dz, sibling)
-
-    def opposite(dz):
+        arrived(shard, part, 10 + 2 * dz)
+        if part == 1:
+            forward(shard, part, 16 + 2 * dz, left)
+        forward(shard, part, 22 + 8 * dz + 2, sibling)
+
+    def opposite(dz, part):
         shard = fs(dz, 2, 0)
-        arrived(shard, 8 + dz, 0)
-        forward(shard, 23 + dz, sibling, 0)
-        arrived(shard, 11 + dz, 1)
-        forward(shard, 26 + dz, sibling, 1)
+        arrived(shard, part, 16 + 2 * dz)
+        forward(shard, part, 22 + 8 * dz + 4, sibling)
 
     def assemble(dz, dx):
         column = ((z + dz) % 3) * 4 + (xx + dx) % 4
@@ -247,38 +298,39 @@
         at = pl.multiple_of(2 * SHARD_ROWS * column, 8)
         nat[pl.ds(at, 2 * SHARD_ROWS), :] = jnp.concatenate(both, axis=0)
 
-    def others(dz):
-        arrived(fs(dz, 0, 1), 14 + dz)
-        assemble(dz, 0)
-        arrived(fs(dz, 3, 1), 17 + dz)
-        assemble(dz, 3)
-        arrived(fs(dz, 1, 1), 20 + dz)
-        assemble(dz, 1)
-        arrived(fs(dz, 2, 1), 23 + dz, 0)
-        arrived(fs(dz, 2, 1), 26 + dz, 1)
-        assemble(dz, 2)
-
-    turn(0)
-    for index, dz in ((0, 2), (1, 1)):
-        shard = fs(dz, 0, 0)
-        arrived(shard, index)
-        forward(shard, 2 + dz, right)
-        forward(shard, 5 + dz, left)
-        forward(shard, 14 + dz, sibling)
-    opposite(0)
-    turn(2)
-    turn(1)
-    others(0)
-    opposite(2)
-    opposite(1)
-
-    each(NT, lambda s: row_in(s).wait_recv())
+    def column(dz, dx):
+        for part in range(2):
+            arrived(fs(dz, dx, 1), part, 22 + 8 * dz + 2 * dx)
+        assemble(dz, dx)
+
+    for part in range(2):
+        turn(0, part)
+    column(0, 0)
+    from_z(0)
+    for part in range(2):
+        opposite(0, part)
+    from_z(1)
+    for dx in (3, 1, 2):
+        column(0, dx)
+    for part in range(2):
+        for dz in (2, 1):
+            turn(dz, part)
+    for dz in (2, 1):
+        column(dz, 0)
+
+    row_in.wait()
     x = nn(by_model[...], arr[...].reshape(NF, 2 * D)).astype(bf16)
     eye = one_hot(iota((2 * D, 2 * D), 0) == iota((2 * D, 2 * D), 1))
     xt = nt(eye, x).astype(bf16)
 
-    others(2)
-    others(1)
+    for part in range(2):
+        for dz in (2, 1):
+            opposite(dz, part)
+    for dz in (2, 1):
+        for dx in (3, 1):
+            column(dz, dx)
+    for dz in (2, 1):
+        column(dz, 2)
 
     lin = jnp.concatenate([nat[pl.ds(q, NLC, stride=4), :] for q in range(4)], axis=1)
     lin = jnp.concatenate([lin, jnp.zeros((16, NF), f32)], axis=0).astype(bf16)
@@ -342,11 +394,24 @@
     wanted = 32 * (at % 8) + at // 8
     wanted = jnp.where(at >= 256, at - 256 + NLC, jnp.where(wanted < NLC, wanted, -1))
     d_rows = nt(one_hot(wanted == iota((272, 256), 1)), d_low)
-    grad_lin = nt(rows(d_rows, 0, 256).astype(bf16), x)
-    lin_msg[...] = jnp.concatenate(
-        [lanes(grad_lin, 0, 256).reshape(NT, 8, 256), lanes(grad_lin, 256, 256).reshape(NT, 8, 256)], axis=1
-    ).astype(bf16)
-    each(NT, lambda s: lin_out(s).start())
+    d_lin = rows(d_rows, 0, 256).astype(bf16)
+
+    def by_owner_rows(v):
+        return jnp.concatenate([lanes(v, 0, 128).reshape(NT, 8, 128), lanes(v, 128, 128).reshape(NT, 8, 128)], axis=1)
+
+    halves = [by_owner_rows(nt(d_lin, rows(x, 256 * core, 256))) for core in range(2)]
+    pair_out[...] = jnp.where(c == 0, halves[1], halves[0]).astype(bf16)
+    kept[...] = jnp.where(c == 0, halves[0], halves[1])
+    swap = pltpu.make_async_remote_copy(
+        src_ref=pair_out,
+        dst_ref=pair_in,
+        send_sem=own_sem.at[0],
+        recv_sem=own_sem.at[1],
+        device_id={"fsdp": sibling},
+        device_id_type=MESH,
+    )
+    swap.start()
+    sent.append(swap)
 
     d_mix = rows(d_rows, 256, 16)
     d_pairs = [
@@ -358,6 +423,30 @@
     d_hidden = nt(d_mixed.astype(bf16), wout[...])
     d_preact = (d_hidden * logistic * (1.0 + preact * (1.0 - logistic))).astype(bf16)
 
+
+    p_lane = iota((NF, NF), 1)
+    to_owner = one_hot(iota((NF, NF), 0) == (p_lane % 16) * 32 + p_lane // 16)
+    by_owner = jnp.concatenate(spread(nn(normed, to_owner), row_mod), axis=0).astype(bf16)
+    at, source = iota((NT * 8, NF), 0), iota((NT * 8, NF), 1)
+    first = nn(one_hot((at // 8 == source // 16) & (at % 8 == (source // 8) % 2)), by_owner)
+    zero = jnp.zeros((2, HID), f32)
+    tile = jnp.concatenate([zero, hidden.astype(f32), zero, zero], axis=0)
+    first = first.reshape(NT, 8, HID) + tile[None]
+    chunks = jnp.concatenate([lanes(d_pairs[b], 128 * q, 128) for b in range(2) for q in range(3)], axis=0)
+    at, source = iota((NT * 8, 48), 0), iota((NT * 8, 48), 1)
+    mine_here = (24 * (at % 8 - 2) + 8 * ((at // 8) % 3) + at // 24 == source) & (at % 8 >= 2) & (at % 8 < 4) & (at < 192)
+    second = nn(one_hot(mine_here), chunks.astype(bf16))
+    tile = jnp.concatenate([d_preact.astype(f32), zero, zero, zero], axis=0)
+    second = second.reshape(NT, 8, HID) + tile[None]
+    fac_msg[...] = jnp.concatenate([first, second], axis=1).astype(bf16)
+    at = iota((NT * 8, NF), 0)
+    slot, owner = at % 8, at // 8
+    wanted = jnp.where((slot == 4) & (owner >= 3), owner - 3, -1)
+    wanted = jnp.where((slot == 5) & (owner >= 3) & (owner <= 5), owner + 26, wanted)
+    proj_place = one_hot(wanted == iota((NT * 8, NF), 1) // 16)
+    swap.wait_recv()
+    lin_msg[...] = (kept[...] + pair_in[...].astype(f32)).astype(bf16)
+    lin_out.start()
     copies = jnp.concatenate(
         [jnp.broadcast_to(d_preact.astype(f32)[b : b + 1], (8, HID)) for b in range(2)], axis=0
     ).astype(bf16)
@@ -370,25 +459,9 @@
 
     grad_proj = nt(d_comp, x).astype(bf16)
     flat = jnp.where(flat_mask, tn(grad_proj, r8), 0.0).astype(bf16)
-    at = iota((64, NF), 0)
-    wanted = jnp.where(
-        at < 32, jnp.where(at >= 3, at - 3, -1), jnp.where((at >= 35) & (at <= 37), at - 6, -1)
-    )
-    proj_out = nn(one_hot(wanted == iota((64, NF), 1) // 16), flat)
-    p_lane = iota((NF, NF), 1)
-    to_owner = one_hot(iota((NF, NF), 0) == (p_lane % 16) * 32 + p_lane // 16)
-    by_owner = spread(nn(normed, to_owner), row_mod)
-    fac[...] = jnp.zeros((NT, 16, 128), f32)
-    fac[:, 2:4] = jnp.broadcast_to(hidden.astype(f32)[None], (NT, 2, HID))
-    fac[:, 8:10] = jnp.broadcast_to(d_preact.astype(f32)[None], (NT, 2, HID))
-    for i in range(NT):
-        fac[i, 0:2] = jnp.sum(by_owner[i].reshape(2, 8, 128), axis=1)
-        fac[i, 4:5] = proj_out[i : i + 1]
-        fac[i, 5:6] = proj_out[32 + i : 33 + i]
-        if i < 24:
-            fac[i, 10:12] = lanes(d_mixed, 128 * i, 128)
-    fac_msg[...] = fac[...].astype(bf16)
-    each(NT, lambda s: fac_out(s).start())
+    proj_rows_out = nn(proj_place, flat).reshape(NT, 8, 128)
+    fac_msg[...] += jnp.concatenate([proj_rows_out, jnp.zeros((NT, 8, 128), f32)], axis=1).astype(bf16)
+    fac_out.start()
 
     left_side = jnp.concatenate([comp, d_comp], axis=0)
     right_side = jnp.concatenate([d_pair, proj_t], axis=0)
@@ -396,17 +469,19 @@
     back[...] = lax.dot_general(
         by_model[...], d_input, (((0,), (1,)), ((), ())), preferred_element_type=f32
     ).astype(bf16).reshape(NT, 16, 2 * D)
-    each(NT, lambda s: row_out(s).start())
 
     got_lin[pl.ds(t, 1)] = lin_msg[pl.ds(t, 1)]
     got_fac[pl.ds(t, 1)] = fac_msg[pl.ds(t, 1)]
     rec_ref[pl.ds(t, 1)] = back[pl.ds(t, 1)]
     out_ref[...] = nt(out_normed.reshape(2 * D, 256).astype(bf16), order[...]).astype(bf16)
+    result = local(out_ref, out_hbm, 5)
+    result.start()
+    locals_started.append(result)
     place = one_hot(iota((NFS * SLOTS, 384), 0) == block_ref[pl.ds(t, 1), :])
 
-    each(NT, lambda s: lin_out(s).wait_recv())
+    lin_out.wait()
     linear = jnp.sum(got_lin[...].astype(f32), axis=0)
-    each(NT, lambda s: fac_out(s).wait_recv())
+    fac_out.wait()
     factors = got_fac[...].astype(f32)
     first = factors[:, 0:8].reshape(NT * 8, 128)
     second = factors[:, 8:16].reshape(NT * 8, 128).astype(bf16)
@@ -417,10 +492,8 @@
     sums = jnp.concatenate(
         [
             products,
-            linear[0:8, 0:128],
-            linear[0:8, 128:256],
-            linear[8:16, 0:128],
-            linear[8:16, 128:256],
+            jnp.where(c == 0, linear, 0.0),
+            jnp.where(c == 1, linear, 0.0),
             tail,
             jnp.zeros((94, 128), f32),
         ],
@@ -428,21 +501,18 @@
     ).astype(bf16)
     blocks[...] = nn(place, sums).astype(bf16).reshape(NFS, SLOTS, 128)
 
-    each(NFS, lambda s: to_fsdp(s).start())
+    to_fsdp.start()
+    row_out.start()
     parts[pl.ds(f, 1)] = blocks[pl.ds(f, 1)]
-    each(NFS, lambda s: to_fsdp(s).wait_recv())
+    to_fsdp.wait()
     mine[...] = jnp.sum(parts[...].astype(f32), axis=0).astype(bf16)
 
-    each(NT, lambda s: all_out(s).start())
+    all_out.start()
     whole_ref[pl.ds(t, 1)] = mine[...][None]
-    each(NT, lambda s: all_out(s).wait_recv())
-    each(NT, lambda s: row_out(s).wait_recv())
-
-    for copy in sent:
-        copy.wait_send()
-    for copies in (row_in, lin_out, fac_out, row_out, all_out):
-        each(NT, lambda s: copies(s).wait_send())
-    each(NFS, lambda s: to_fsdp(s).wait_send())
+    all_out.wait()
+    row_out.wait()
+
+    drain()
 
 
 def finish_kernel(out_ref, rec_ref, whole_ref, row_ref, layer_ref, emb_ref, grad_ref):
@@ -455,6 +525,7 @@
 
 
 VMEM = pl.BlockSpec(memory_space=pltpu.VMEM)
+IN_HBM = pl.BlockSpec(memory_space=pltpu.HBM)
 LIMIT = 40 * 1024 * 1024
 
 
@@ -466,9 +537,15 @@
     return pl.pallas_call(
         whole_kernel,
         out_shape=(shape(bf16, 2 * D, 256), shape(bf16, NT, 16, 2 * D), shape(bf16, NT, SLOTS, 128)),
-        in_specs=[VMEM] * 5,
-        out_specs=(VMEM,) * 3,
+        in_specs=[IN_HBM] * 5,
+        out_specs=(IN_HBM, VMEM, VMEM),
         scratch_shapes=[
+            pltpu.VMEM((NT, 2, 16, D), bf16),
+            pltpu.VMEM((SHARD_ROWS, 128), bf16),
+            pltpu.VMEM((1, NF), jnp.int32),
+            pltpu.VMEM((2 * D, 256), bf16),
+            pltpu.VMEM((NT, 384), jnp.int32),
+            pltpu.VMEM((2 * D, 256), bf16),
             pltpu.VMEM((NT, 16, 2 * D), bf16),
             pltpu.VMEM((PIECE_ROWS, 128), bf16),
             pltpu.VMEM((NT, 16, 2 * D), bf16),
@@ -478,20 +555,26 @@
             pltpu.VMEM((NF, NF), bf16),
             pltpu.VMEM((256, 256), bf16),
             pltpu.VMEM((2 * D, 256), f32),
-            pltpu.VMEM((NT, 16, 256), bf16),
+            pltpu.VMEM((NT, 16, 128), bf16),
+            pltpu.VMEM((NT, 16, 128), bf16),
+            pltpu.VMEM((NT, 16, 128), f32),
+            pltpu.VMEM((NT, 16, 128), bf16),
             pltpu.VMEM((NT, 16, 128), bf16),
             pltpu.VMEM((NT, 16, 2 * D), bf16),
-            pltpu.VMEM((NT, 16, 128), f32),
-            pltpu.VMEM((NT, 16, 256), bf16),
+            pltpu.VMEM((NT, 16, 128), bf16),
             pltpu.VMEM((NT, 16, 128), bf16),
             pltpu.VMEM((NFS, SLOTS, 128), bf16),
             pltpu.VMEM((NFS, SLOTS, 128), bf16),
             pltpu.VMEM((SLOTS, 128), bf16),
             pltpu.SemaphoreType.DMA((2,)),
-        ]
-        + [pltpu.SemaphoreType.DMA((NT,))] * 14,
+            pltpu.SemaphoreType.DMA((6,)),
+            pltpu.SemaphoreType.DMA((46,)),
+            pltpu.SemaphoreType.DMA((46,)),
+            pltpu.SemaphoreType.DMA((6,)),
+            pltpu.SemaphoreType.DMA((6,)),
+        ],
         compiler_params=pltpu.CompilerParams(collective_id=0, has_side_effects=True, vmem_limit_bytes=LIMIT),
-    )(looked, shard, as_row, cotangent, jnp.asarray(TO_BLOCK))
+    )(*[pltpu.with_memory_space_constraint(v, pltpu.HBM) for v in (looked, shard, as_row, cotangent, jnp.asarray(TO_BLOCK))])
 
 
 def finish(out, rec, gathered):
@@ -500,6 +583,7 @@
         out_shape=(shape(bf16, 2 * D, 256), shape(bf16, NT, 2, 16, D), shape(f32, SHARD_ROWS, 128)),
         in_specs=[VMEM] * 4,
         out_specs=(VMEM,) * 3,
+        compiler_params=pltpu.CompilerParams(vmem_limit_bytes=12 * 1024 * 1024),
     )(out, rec, gathered, jnp.asarray(TO_ROW))
 
 

time: 88.9 us -> 73.4 us (0.83)
  Pallas kernels: 80.9 us -> 72.5 us
  local copies, waits for them, and re-layouts: 6.37 us -> 0.01 us
    pallas_call x1, Pallas kernels: 78.7 us -> 71.4 us  [whole(): pl.pallas_call(whole_kernel, out_shape=(shape(bf16, 2 * D, 256), shape(bf...]
    unnamed x16 -> x2, local copies, waits for them, and re-layouts: 6.37 us -> 0.01 us
    pallas_call x1, Pallas kernels: 2.23 us -> 1.12 us  [finish(): pl.pallas_call(finish_kernel, out_shape=(shape(bf16, 2 * D, 256), shape(b...]
where the time goes in v3:
time: 73.4 us; the launch traced here: 73.2 us
  Pallas kernels  72.5 us (99%)
    pallas_call x1, Pallas kernels, whole(): pl.pallas_call(whole_kernel, out_shape=(shape(bf16, 2 * D, 256), shape(bf...  71.4 us

profile of v3, /device:TPU:6, one launch (start us, length us, event | category | flops | bytes accessed | tf_op | source)
XLA Modules:
  0.0 73.2 jit_solution(13681028864462423038)
XLA Ops:
  0.6 0.0 copy-start
  0.6 71.4 %shard_map.85 = (bf16[384,256]{1,0:T(8,128)(2,1)S(1)}, bf16[32,16,384]{2,1,0:T(8,128)(2,1)S(1)}, bf16[32,16,128]{2,1,0:T(8,128)(2,1)S(1)}) custom-call(bf16[32,2,16,192]{3,2,1,0:T(8,128)(2,1)} %bitcast.11, bf16[340,128]{1,0:T(8,128)(2,1)} %bitcast.13, s32[1,512]{1,0:T(1,128)} %bitcast.14, bf16[384,256]{1,0:T(8,128)(2,1)} %bitcast.12, ...), custom_call_target="tpu_custom_call" | custom-call | tf_op jit(solution)/shard_map/pallas_call | solution.py:537
  72.1 0.0 copy-done
  72.1 1.1 %shard_map.86 = (bf16[384,256]{1,0:T(8,128)(2,1)}, bf16[32,2,16,192]{3,2,1,0:T(8,128)(2,1)}, f32[340,128]{1,0:T(8,128)}) custom-call(bf16[384,256]{1,0:T(8,128)(2,1)S(1)} %get-tuple-element.9.out_ref, bf16[32,16,384]{2,1,0:T(8,128)(2,1)S(1)} %get-tuple-element.10.rec_ref, bf16[32,16,128]{2,1,0:T(8,128)(2,1)S(1)} %get-tuple-element.11.whole_ref, ...), custom_call_target="tpu_custom_call" | custom-call | tf_op jit(solution)/shard_map/pallas_call | solution.py:581
Async XLA Ops:
  0.6 71.4 %copy-start = (s32[24,512]{1,0:T(8,128)S(1)}, s32[24,512]{1,0:T(8,128)}, u32[]{:S(2)}) copy-start(s32[24,512]{1,0:T(8,128)} %constant.5.clone.row_ref) | copy-start | bytes 147460

commit v4 on v3

--- a/solution.py
+++ b/solution.py
@@ -16,6 +16,7 @@
 NLC = 240
 NT = 32
 NFS = 24
+PROJ_F = 2
 SHARD_ROWS = 340
 PIECE_ROWS = 352
 HALF_ROWS = PIECE_ROWS // 2
@@ -43,10 +44,6 @@
             for m in range(8):
                 if 32 * m + t < NLC:
                     owned[t].append((4 * (32 * m + t) + q, 256 + q * 8 + m))
-        if t >= 3:
-            owned[t].append((PROJ_ROW + t - 3, 288))
-        if 3 <= t <= 5:
-            owned[t].append((PROJ_ROW + 26 + t, 289))
     to_block = np.full((NT, 384), -1, np.int32)
     to_row = np.full((NFS, NT * SLOTS), -1, np.int32)
     seen = 0
@@ -60,7 +57,7 @@
             to_block[t, place] = f * SLOTS + slot
             to_row[f, t * SLOTS + slot] = row - f * SHARD_ROWS
             seen += 1
-    assert seen == TOTAL_ROWS
+    assert seen == TOTAL_ROWS - 32
     return to_block, to_row
 
 
@@ -120,10 +117,10 @@
 
 
 def whole_kernel(
-    lk_hbm, w_hbm, as_row_hbm, cot_hbm, block_hbm, out_hbm, rec_ref, whole_ref,
-    lk_ref, w_ref, as_row_ref, cot_ref, block_ref, out_ref, pack, padded, arr, all_ref, nat, wout, by_model, order, upstream, pair_out, pair_in, kept, lin_msg, fac_msg, back,
-    got_lin, got_fac, blocks, parts, mine,
-    own_sem, in_sem, w_send, w_recv, ex_send, ex_recv,
+    lk_hbm, w_hbm, as_row_hbm, cot_hbm, block_hbm, out_hbm, rec_ref, whole_ref, proj_all,
+    lk_ref, w_ref, as_row_ref, cot_ref, block_ref, out_ref, pack, padded, arr, all_ref, nat, wout, by_model, order, upstream, to_owner, owner_sum, mixed_place, linear_place, block_place, pair_out, pair_in, kept, lin_msg, fac_msg, back,
+    got_lin, got_fac, blocks, parts, mine, proj_mine, proj_parts, proj_sum,
+    own_sem, in_sem, proj_sem, w_send, w_recv, ex_send, ex_recv,
 ):
     t = lax.axis_index("table")
     f = lax.axis_index("fsdp")
@@ -132,12 +129,12 @@
     def fs(dz, dx, dc):
         return ((z + dz) % 3) * 8 + ((xx + dx) % 4) * 2 + (c + dc) % 2
 
-    def each(n, act):
+    def each(n, act, first=1):
         def step(s, carry):
             act(s)
             return carry
 
-        lax.fori_loop(1, n, step, 0)
+        lax.fori_loop(first, n, step, 0)
 
     class Exchange:
         def __init__(self, axis, src, dst, index):
@@ -146,7 +143,7 @@
             def copy(s):
                 to = (me + s) % self.n
                 return pltpu.make_async_remote_copy(
-                    src_ref=src if src is mine else src.at[to],
+                    src_ref=src.at[to] if len(src.shape) == len(dst.shape) else src,
                     dst_ref=dst.at[me],
                     send_sem=ex_send.at[index],
                     recv_sem=ex_recv.at[index],
@@ -184,9 +181,23 @@
     row_out = Exchange("table", back, rec_ref, 3)
     all_out = Exchange("table", mine, whole_ref, 4)
     to_fsdp = Exchange("fsdp", blocks, parts, 5)
+    proj_bcast = Exchange("table", proj_sum, proj_all, 6)
 
     def local(src, dst, index):
         return pltpu.make_async_copy(src, dst, in_sem.at[index])
+
+    barrier = pltpu.get_barrier_semaphore()
+    near = (fs(1, 0, 0), fs(2, 0, 0), fs(0, 1, 0), fs(0, 3, 0), fs(0, 0, 1))
+
+    def greet(axis, to):
+        pl.semaphore_signal(barrier, inc=1, device_id={axis: to}, device_id_type=MESH)
+
+    greet("fsdp", near[0])
+    greet("fsdp", near[1])
+    for low, high in ((12, 21), (6, 12), (21, 27), (1, 6), (27, NT)):
+        each(high, lambda s: greet("table", (t + s) % NT), low)
+    for other in near[2:]:
+        greet("fsdp", other)
 
     inputs = [
         local(w_hbm, w_ref, 0),
@@ -198,11 +209,6 @@
     for copy in inputs:
         copy.start()
 
-    barrier = pltpu.get_barrier_semaphore()
-    near = (fs(1, 0, 0), fs(2, 0, 0), fs(0, 1, 0), fs(0, 3, 0), fs(0, 0, 1))
-    each(NT, lambda s: pl.semaphore_signal(barrier, inc=1, device_id={"table": (t + s) % NT}, device_id_type=MESH))
-    for other in near:
-        pl.semaphore_signal(barrier, inc=1, device_id={"fsdp": other}, device_id_type=MESH)
     inputs[0].wait()
     padded[0:SHARD_ROWS] = w_ref[...]
     padded[SHARD_ROWS:PIECE_ROWS] = jnp.zeros((PIECE_ROWS - SHARD_ROWS, 128), bf16)
@@ -306,6 +312,19 @@
     for part in range(2):
         turn(0, part)
     column(0, 0)
+
+    p_lane = iota((NF, NF), 1)
+    to_owner[...] = one_hot(iota((NF, NF), 0) == (p_lane % 16) * 32 + p_lane // 16)
+    at, source = iota((NT * 8, NF), 0), iota((NT * 8, NF), 1)
+    owner_sum[...] = one_hot((at // 8 == source // 16) & (at % 8 == (source // 8) % 2))
+    at, source = iota((NT * 8, 48), 0), iota((NT * 8, 48), 1)
+    mine_here = (24 * (at % 8 - 2) + 8 * ((at // 8) % 3) + at // 24 == source) & (at % 8 >= 2) & (at % 8 < 4) & (at < 192)
+    mixed_place[...] = one_hot(mine_here)
+    at = iota((256, 256), 0)
+    wanted = 32 * (at % 8) + at // 8
+    linear_place[...] = one_hot(jnp.where(wanted < NLC, wanted, -1) == iota((256, 256), 1))
+    block_place[...] = one_hot(iota((NFS * SLOTS, 384), 0) == block_ref[pl.ds(t, 1), :])
+
     from_z(0)
     for part in range(2):
         opposite(0, part)
@@ -334,67 +353,17 @@
 
     lin = jnp.concatenate([nat[pl.ds(q, NLC, stride=4), :] for q in range(4)], axis=1)
     lin = jnp.concatenate([lin, jnp.zeros((16, NF), f32)], axis=0).astype(bf16)
-    for chunk in range(24):
-        wout[:, 128 * chunk : 128 * chunk + 128] = nat[pl.ds(OUT_ROW + chunk, HID, stride=24), :].astype(bf16)
-    proj_rows = nat[PROJ_ROW : PROJ_ROW + 32, :].astype(bf16)
-    up = nat[UP_ROW : UP_ROW + NF * RANK, :].astype(bf16)
-
-    r8 = one_hot(iota((8, 128), 1) % 8 == iota((8, 128), 0))
-    flat_mask = iota((NF, 128), 1) // 8 == iota((NF, 128), 0) % 16
-    picked = nn(one_hot(iota((NF, 32), 1) == iota((NF, 32), 0) // 16), proj_rows)
-    picked = jnp.where(flat_mask, picked, 0.0).astype(bf16)
-    proj_t = nt(r8, picked).astype(bf16)
-
-    half = iota((16, 2 * D), 1) // D == iota((16, 2 * D), 0) // 8
-    comp = nn(proj_t, x)
-    comp = jnp.concatenate([comp, comp], axis=0)
-    comp = jnp.where(half, comp, 0.0).astype(bf16)
-    pair = nt(comp, x)
-
-    def per_sample(v):
-        total = jnp.sum(v.reshape(2, 8, NF), axis=(1, 2), keepdims=True) * (1.0 / (NF * RANK))
-        return jnp.broadcast_to(total, (2, 8, NF)).reshape(16, NF)
-
-    centred = pair - per_sample(pair)
-    pair_scale = lax.rsqrt(per_sample(centred * centred) + 1e-05)
-    normed_full = centred * pair_scale
-    normed = normed_full.astype(bf16)
-    row_mod = iota((16, 128), 0) % 8
-    wide = jnp.concatenate(spread(normed.astype(f32), row_mod), axis=1).astype(bf16)
-    preact = jnp.sum(nn(wide, up).reshape(2, 8, HID), axis=1)
-    logistic = 1.0 / (1.0 + jnp.exp(-preact))
-    hidden = (preact / (1.0 + jnp.exp(-preact))).astype(bf16)
-    mixed = nn(hidden, wout[...])
-
-    def by_pairs(b):
-        return jnp.concatenate([lanes(mixed[b : b + 1], 384 * e, 384) for e in range(8)], axis=0)
-
-    m0, m1 = by_pairs(0), by_pairs(1)
-    mix = jnp.concatenate(
-        [
-            jnp.concatenate([lanes(m0, 0, D), lanes(m1, 0, D)], axis=1),
-            jnp.concatenate([lanes(m0, D, D), lanes(m1, D, D)], axis=1),
-        ],
-        axis=0,
-    )
-    mix = jnp.concatenate([jnp.zeros((112, 2 * D), f32), mix], axis=0).T
-    linear = nt(xt, lin)
-    joined = jnp.concatenate([lanes(linear, 0, 128), lanes(linear, 128, 128) + mix], axis=1)
-
-    joined = joined.reshape(2, D, 256)
-    mean = lambda v: jnp.mean(v, axis=1, keepdims=True)
-    centred_out = joined - mean(joined)
-    out_scale = lax.rsqrt(mean(centred_out * centred_out) + 1e-05)
-    out_normed = centred_out * out_scale
-    cot = upstream[...].reshape(2, D, 256)
-    d_low = out_scale * (cot - mean(cot) - out_normed * mean(cot * out_normed))
-    d_low = d_low.reshape(2 * D, 256).astype(bf16)
-
-    at = iota((272, 256), 0)
-    wanted = 32 * (at % 8) + at // 8
-    wanted = jnp.where(at >= 256, at - 256 + NLC, jnp.where(wanted < NLC, wanted, -1))
-    d_rows = nt(one_hot(wanted == iota((272, 256), 1)), d_low)
-    d_lin = rows(d_rows, 0, 256).astype(bf16)
+    def normalise(v, c):
+        v, c = v.reshape(2, D, -1), c.reshape(2, D, -1)
+        mean = lambda u: jnp.mean(u, axis=1, keepdims=True)
+        centred_v = v - mean(v)
+        scale = lax.rsqrt(mean(centred_v * centred_v) + 1e-05)
+        n = centred_v * scale
+        d = scale * (c - mean(c) - n * mean(c * n))
+        return n.reshape(2 * D, -1).astype(bf16), d.reshape(2 * D, -1).astype(bf16)
+
+    linear_out, d_linear = normalise(nt(xt, lin), upstream[...])
+    d_lin = nt(linear_place[...], d_linear).astype(bf16)
 
     def by_owner_rows(v):
         return jnp.concatenate([lanes(v, 0, 128).reshape(NT, 8, 128), lanes(v, 128, 128).reshape(NT, 8, 128)], axis=1)
@@ -413,7 +382,63 @@
     swap.start()
     sent.append(swap)
 
-    d_mix = rows(d_rows, 256, 16)
+    for chunk in range(24):
+        wout[:, 128 * chunk : 128 * chunk + 128] = nat[pl.ds(OUT_ROW + chunk, HID, stride=24), :].astype(bf16)
+    proj_rows = nat[PROJ_ROW : PROJ_ROW + 32, :].astype(bf16)
+    up = nat[UP_ROW : UP_ROW + NF * RANK, :].astype(bf16)
+
+    swap.wait_recv()
+    lin_msg[...] = (kept[...] + pair_in[...].astype(f32)).astype(bf16)
+    lin_out.start()
+
+    r8 = one_hot(iota((8, 128), 1) % 8 == iota((8, 128), 0))
+    flat_mask = iota((NF, 128), 1) // 8 == iota((NF, 128), 0) % 16
+    picked = nn(one_hot(iota((NF, 32), 1) == iota((NF, 32), 0) // 16), proj_rows)
+    picked = jnp.where(flat_mask, picked, 0.0).astype(bf16)
+    proj_t = nt(r8, picked).astype(bf16)
+
+    half = iota((16, 2 * D), 1) // D == iota((16, 2 * D), 0) // 8
+    comp = nn(proj_t, x)
+    comp = jnp.concatenate([comp, comp], axis=0)
+    comp = jnp.where(half, comp, 0.0).astype(bf16)
+    pair = nt(comp, x)
+
+    def per_sample(v):
+        total = jnp.sum(v.reshape(2, 8, NF), axis=(1, 2), keepdims=True) * (1.0 / (NF * RANK))
+        return jnp.broadcast_to(total, (2, 8, NF)).reshape(16, NF)
+
+    centred = pair - per_sample(pair)
+    pair_scale = lax.rsqrt(per_sample(centred * centred) + 1e-05)
+    normed_full = centred * pair_scale
+    normed = normed_full.astype(bf16)
+    row_mod = iota((16, 128), 0) % 8
+    wide = jnp.concatenate(spread(normed.astype(f32), row_mod), axis=1).astype(bf16)
+    preact = jnp.sum(nn(wide, up).reshape(2, 8, HID), axis=1)
+    logistic = 1.0 / (1.0 + jnp.exp(-preact))
+    hidden = (preact / (1.0 + jnp.exp(-preact))).astype(bf16)
+    mixed = nn(hidden, wout[...])
+
+    def by_pairs(b):
+        return jnp.concatenate([lanes(mixed[b : b + 1], 384 * e, 384) for e in range(8)], axis=0)
+
+    m0, m1 = by_pairs(0), by_pairs(1)
+    mix = jnp.concatenate(
+        [
+            jnp.concatenate([lanes(m0, 0, D), lanes(m1, 0, D)], axis=1),
+            jnp.concatenate([lanes(m0, D, D), lanes(m1, D, D)], axis=1),
+        ],
+        axis=0,
+    )
+    mix = jnp.concatenate([jnp.zeros((112, 2 * D), f32), mix], axis=0).T
+    mixed_out, d_mix = normalise(mix, lanes(upstream[...], 128, 128))
+    late = iota((2 * D, 128), 1) >= 112
+
+    def join(a, b):
+        high = jnp.where(late, b.astype(f32), lanes(a, 128, 128).astype(f32)).astype(bf16)
+        return jnp.concatenate([lanes(a, 0, 128), high], axis=1)
+
+    d_low = join(d_linear, d_mix)
+    d_mix = nt(one_hot(iota((16, 128), 1) == iota((16, 128), 0) + 112), d_mix)
     d_pairs = [
         jnp.concatenate([lanes(d_mix[0:8], b * D, D), lanes(d_mix[8:16], b * D, D)], axis=1) for b in range(2)
     ]
@@ -424,29 +449,18 @@
     d_preact = (d_hidden * logistic * (1.0 + preact * (1.0 - logistic))).astype(bf16)
 
 
-    p_lane = iota((NF, NF), 1)
-    to_owner = one_hot(iota((NF, NF), 0) == (p_lane % 16) * 32 + p_lane // 16)
-    by_owner = jnp.concatenate(spread(nn(normed, to_owner), row_mod), axis=0).astype(bf16)
-    at, source = iota((NT * 8, NF), 0), iota((NT * 8, NF), 1)
-    first = nn(one_hot((at // 8 == source // 16) & (at % 8 == (source // 8) % 2)), by_owner)
+    by_owner = jnp.concatenate(spread(nn(normed, to_owner[...]), row_mod), axis=0).astype(bf16)
+    first = nn(owner_sum[...], by_owner)
     zero = jnp.zeros((2, HID), f32)
     tile = jnp.concatenate([zero, hidden.astype(f32), zero, zero], axis=0)
     first = first.reshape(NT, 8, HID) + tile[None]
     chunks = jnp.concatenate([lanes(d_pairs[b], 128 * q, 128) for b in range(2) for q in range(3)], axis=0)
-    at, source = iota((NT * 8, 48), 0), iota((NT * 8, 48), 1)
-    mine_here = (24 * (at % 8 - 2) + 8 * ((at // 8) % 3) + at // 24 == source) & (at % 8 >= 2) & (at % 8 < 4) & (at < 192)
-    second = nn(one_hot(mine_here), chunks.astype(bf16))
+    second = nn(mixed_place[...], chunks.astype(bf16))
     tile = jnp.concatenate([d_preact.astype(f32), zero, zero, zero], axis=0)
     second = second.reshape(NT, 8, HID) + tile[None]
     fac_msg[...] = jnp.concatenate([first, second], axis=1).astype(bf16)
-    at = iota((NT * 8, NF), 0)
-    slot, owner = at % 8, at // 8
-    wanted = jnp.where((slot == 4) & (owner >= 3), owner - 3, -1)
-    wanted = jnp.where((slot == 5) & (owner >= 3) & (owner <= 5), owner + 26, wanted)
-    proj_place = one_hot(wanted == iota((NT * 8, NF), 1) // 16)
-    swap.wait_recv()
-    lin_msg[...] = (kept[...] + pair_in[...].astype(f32)).astype(bf16)
-    lin_out.start()
+    fac_out.start()
+
     copies = jnp.concatenate(
         [jnp.broadcast_to(d_preact.astype(f32)[b : b + 1], (8, HID)) for b in range(2)], axis=0
     ).astype(bf16)
@@ -459,9 +473,20 @@
 
     grad_proj = nt(d_comp, x).astype(bf16)
     flat = jnp.where(flat_mask, tn(grad_proj, r8), 0.0).astype(bf16)
-    proj_rows_out = nn(proj_place, flat).reshape(NT, 8, 128)
-    fac_msg[...] += jnp.concatenate([proj_rows_out, jnp.zeros((NT, 8, 128), f32)], axis=1).astype(bf16)
-    fac_out.start()
+    proj_mine[...] = nn(one_hot(iota((32, NF), 1) // 16 == iota((32, NF), 0)), flat).astype(bf16)
+    proj_out = pltpu.make_async_remote_copy(
+        src_ref=proj_mine,
+        dst_ref=proj_parts.at[f],
+        send_sem=proj_sem.at[0],
+        recv_sem=proj_sem.at[1],
+        device_id={"fsdp": PROJ_F},
+        device_id_type=MESH,
+    )
+
+    @pl.when(f != PROJ_F)
+    def _():
+        proj_out.start()
+        proj_all[...] = jnp.zeros_like(proj_all)
 
     left_side = jnp.concatenate([comp, d_comp], axis=0)
     right_side = jnp.concatenate([d_pair, proj_t], axis=0)
@@ -473,11 +498,10 @@
     got_lin[pl.ds(t, 1)] = lin_msg[pl.ds(t, 1)]
     got_fac[pl.ds(t, 1)] = fac_msg[pl.ds(t, 1)]
     rec_ref[pl.ds(t, 1)] = back[pl.ds(t, 1)]
-    out_ref[...] = nt(out_normed.reshape(2 * D, 256).astype(bf16), order[...]).astype(bf16)
+    out_ref[...] = nt(join(linear_out, mixed_out), order[...]).astype(bf16)
     result = local(out_ref, out_hbm, 5)
     result.start()
     locals_started.append(result)
-    place = one_hot(iota((NFS * SLOTS, 384), 0) == block_ref[pl.ds(t, 1), :])
 
     lin_out.wait()
     linear = jnp.sum(got_lin[...].astype(f32), axis=0)
@@ -488,21 +512,36 @@
     at = iota((NT * 8, 128), 0) % 8
     left_side = jnp.concatenate([jnp.where(at < 2, first, 0.0), jnp.where((at == 2) | (at == 3), first, 0.0)], axis=1)
     products = tn(left_side.astype(bf16), second)
-    tail = jnp.sum(factors[:, 0:8], axis=0)[4:6]
     sums = jnp.concatenate(
         [
             products,
             jnp.where(c == 0, linear, 0.0),
             jnp.where(c == 1, linear, 0.0),
-            tail,
-            jnp.zeros((94, 128), f32),
+            jnp.zeros((96, 128), f32),
         ],
         axis=0,
     ).astype(bf16)
-    blocks[...] = nn(place, sums).astype(bf16).reshape(NFS, SLOTS, 128)
+    blocks[...] = nn(block_place[...], sums).astype(bf16).reshape(NFS, SLOTS, 128)
 
     to_fsdp.start()
     row_out.start()
+
+    @pl.when(f == PROJ_F)
+    def _():
+        others = proj_parts.at[pl.ds(0, NFS - 1)]
+        pltpu.make_async_remote_copy(
+            src_ref=others,
+            dst_ref=others,
+            send_sem=proj_sem.at[0],
+            recv_sem=proj_sem.at[1],
+            device_id={"fsdp": f},
+            device_id_type=MESH,
+        ).wait_recv()
+        proj_parts[pl.ds(f, 1)] = proj_mine[...][None]
+        proj_sum[...] = jnp.sum(proj_parts[...].astype(f32), axis=0).astype(bf16)
+        each(NT, lambda s: proj_bcast.copy(s).start())
+        proj_all[pl.ds(t, 1)] = proj_sum[...][None]
+
     parts[pl.ds(f, 1)] = blocks[pl.ds(f, 1)]
     to_fsdp.wait()
     mine[...] = jnp.sum(parts[...].astype(f32), axis=0).astype(bf16)
@@ -512,10 +551,19 @@
     all_out.wait()
     row_out.wait()
 
+    @pl.when(f == PROJ_F)
+    def _():
+        proj_bcast.wait()
+        proj_bcast.wait_send()
+
+    @pl.when(f != PROJ_F)
+    def _():
+        proj_out.wait_send()
+
     drain()
 
 
-def finish_kernel(out_ref, rec_ref, whole_ref, row_ref, layer_ref, emb_ref, grad_ref):
+def finish_kernel(out_ref, rec_ref, whole_ref, proj_ref, row_ref, layer_ref, emb_ref, grad_ref):
     f = lax.axis_index("fsdp")
     layer_ref[...] = out_ref[...]
     emb_ref[:, 0] = rec_ref[:, :, 0:D]
@@ -523,6 +571,11 @@
     final = one_hot(iota((SHARD_ROWS, NT * SLOTS), 0) == row_ref[pl.ds(f, 1), :])
     grad_ref[...] = nn(final, whole_ref[...].reshape(NT * SLOTS, 128)) * (1.0 / SAMPLES)
 
+    @pl.when(f == PROJ_F)
+    def _():
+        at = pl.ds(PROJ_ROW - PROJ_F * SHARD_ROWS, 32)
+        grad_ref[at, :] = jnp.sum(proj_ref[...].astype(f32), axis=0) * (1.0 / SAMPLES)
+
 
 VMEM = pl.BlockSpec(memory_space=pltpu.VMEM)
 IN_HBM = pl.BlockSpec(memory_space=pltpu.HBM)
@@ -536,9 +589,14 @@
 def whole(looked, shard, as_row, cotangent):
     return pl.pallas_call(
         whole_kernel,
-        out_shape=(shape(bf16, 2 * D, 256), shape(bf16, NT, 16, 2 * D), shape(bf16, NT, SLOTS, 128)),
+        out_shape=(
+            shape(bf16, 2 * D, 256),
+            shape(bf16, NT, 16, 2 * D),
+            shape(bf16, NT, SLOTS, 128),
+            shape(bf16, NT, 32, 128),
+        ),
         in_specs=[IN_HBM] * 5,
-        out_specs=(IN_HBM, VMEM, VMEM),
+        out_specs=(IN_HBM, VMEM, VMEM, VMEM),
         scratch_shapes=[
             pltpu.VMEM((NT, 2, 16, D), bf16),
             pltpu.VMEM((SHARD_ROWS, 128), bf16),
@@ -555,6 +613,11 @@
             pltpu.VMEM((NF, NF), bf16),
             pltpu.VMEM((256, 256), bf16),
             pltpu.VMEM((2 * D, 256), f32),
+            pltpu.VMEM((NF, NF), bf16),
+            pltpu.VMEM((NT * 8, NF), bf16),
+            pltpu.VMEM((NT * 8, 48), bf16),
+            pltpu.VMEM((256, 256), bf16),
+            pltpu.VMEM((NFS * SLOTS, 384), bf16),
             pltpu.VMEM((NT, 16, 128), bf16),
             pltpu.VMEM((NT, 16, 128), bf16),
             pltpu.VMEM((NT, 16, 128), f32),
@@ -566,35 +629,39 @@
             pltpu.VMEM((NFS, SLOTS, 128), bf16),
             pltpu.VMEM((NFS, SLOTS, 128), bf16),
             pltpu.VMEM((SLOTS, 128), bf16),
+            pltpu.VMEM((32, 128), bf16),
+            pltpu.VMEM((NFS, 32, 128), bf16),
+            pltpu.VMEM((32, 128), bf16),
             pltpu.SemaphoreType.DMA((2,)),
             pltpu.SemaphoreType.DMA((6,)),
+            pltpu.SemaphoreType.DMA((2,)),
             pltpu.SemaphoreType.DMA((46,)),
             pltpu.SemaphoreType.DMA((46,)),
-            pltpu.SemaphoreType.DMA((6,)),
-            pltpu.SemaphoreType.DMA((6,)),
+            pltpu.SemaphoreType.DMA((7,)),
+            pltpu.SemaphoreType.DMA((7,)),
         ],
         compiler_params=pltpu.CompilerParams(collective_id=0, has_side_effects=True, vmem_limit_bytes=LIMIT),
     )(*[pltpu.with_memory_space_constraint(v, pltpu.HBM) for v in (looked, shard, as_row, cotangent, jnp.asarray(TO_BLOCK))])
 
 
-def finish(out, rec, gathered):
+def finish(out, rec, gathered, proj):
     return pl.pallas_call(
         finish_kernel,
         out_shape=(shape(bf16, 2 * D, 256), shape(bf16, NT, 2, 16, D), shape(f32, SHARD_ROWS, 128)),
-        in_specs=[VMEM] * 4,
+        in_specs=[VMEM] * 5,
         out_specs=(VMEM,) * 3,
         compiler_params=pltpu.CompilerParams(vmem_limit_bytes=12 * 1024 * 1024),
-    )(out, rec, gathered, jnp.asarray(TO_ROW))
+    )(out, rec, gathered, proj, jnp.asarray(TO_ROW))
 
 
 def shards(looked_up, assignment, flat_weights, cotangent):
-    out, rec, gathered = whole(
+    out, rec, gathered, proj = whole(
         looked_up.reshape(NT, 2, 16, D),
         flat_weights.reshape(SHARD_ROWS, 128),
         assignment.reshape(1, NF),
         cotangent.transpose(0, 2, 1).reshape(2 * D, 256),
     )
-    layer_out, emb, grad = finish(out, rec, gathered)
+    layer_out, emb, grad = finish(out, rec, gathered, proj)
     return layer_out.reshape(2, D, 256).transpose(0, 2, 1), emb.reshape(2 * NT, 16, D), grad.reshape(SHARD_ROWS * 128)
 
 

time: 73.4 us -> 74.1 us (level)
  the two profiles are of different devices: /device:TPU:6 before, /device:TPU:2 now
where the time goes in v4:
time: 74.1 us; the launch traced here: 74 us
  Pallas kernels  73.3 us (99%)
    pallas_call x1, Pallas kernels, whole(): pl.pallas_call(whole_kernel, out_shape=(shape(bf16, 2 * D, 256), shape(bf...  72.1 us

profile of v4, /device:TPU:2, one launch (start us, length us, event | category | flops | bytes accessed | tf_op | source)
XLA Modules:
  0.0 74.0 jit_solution(6823380500670027856)
XLA Ops:
  0.6 0.0 copy-start
  0.6 72.1 %shard_map.85 = (bf16[384,256]{1,0:T(8,128)(2,1)S(1)}, bf16[32,16,384]{2,1,0:T(8,128)(2,1)S(1)}, bf16[32,16,128]{2,1,0:T(8,128)(2,1)S(1)}, bf16[32,32,128]{2,1,0:T(8,128)(2,1)S(1)}) custom-call(bf16[32,2,16,192]{3,2,1,0:T(8,128)(2,1)} %bitcast.11, bf16[340,128]{1,0:T(8,128)(2,1)} %bitcast.13, s32[1,512]{1,0:T(1,128)} %bitcast.14, bf16[384,256]{1,0:T(8,128)(2,1)} %bitcast.12, ...), custom_call_target="tpu_custom_call" | custom-call | tf_op jit(solution)/shard_map/pallas_call | solution.py:590
  72.7 0.0 copy-done
  72.7 1.2 %shard_map.86 = (bf16[384,256]{1,0:T(8,128)(2,1)}, bf16[32,2,16,192]{3,2,1,0:T(8,128)(2,1)}, f32[340,128]{1,0:T(8,128)}) custom-call(bf16[384,256]{1,0:T(8,128)(2,1)S(1)} %get-tuple-element.10.out_ref, bf16[32,16,384]{2,1,0:T(8,128)(2,1)S(1)} %get-tuple-element.11.rec_ref, bf16[32,16,128]{2,1,0:T(8,128)(2,1)S(1)} %get-tuple-element.12.whole_ref, ...), custom_call_target="tpu_custom_call" | custom-call | tf_op jit(solution)/shard_map/pallas_call | solution.py:648
Async XLA Ops:
  0.6 72.1 %copy-start = (s32[24,512]{1,0:T(8,128)S(1)}, s32[24,512]{1,0:T(8,128)}, u32[]{:S(2)}) copy-start(s32[24,512]{1,0:T(8,128)} %constant.5.clone.row_ref) | copy-start | bytes 147460

commit v5 on v4

--- a/solution.py
+++ b/solution.py
@@ -119,12 +119,13 @@
 def whole_kernel(
     lk_hbm, w_hbm, as_row_hbm, cot_hbm, block_hbm, out_hbm, rec_ref, whole_ref, proj_all,
     lk_ref, w_ref, as_row_ref, cot_ref, block_ref, out_ref, pack, padded, arr, all_ref, nat, wout, by_model, order, upstream, to_owner, owner_sum, mixed_place, linear_place, block_place, pair_out, pair_in, kept, lin_msg, fac_msg, back,
-    got_lin, got_fac, blocks, parts, mine, proj_mine, proj_parts, proj_sum,
-    own_sem, in_sem, proj_sem, w_send, w_recv, ex_send, ex_recv,
+    got_lin, got_fac, blocks, parts, mine, proj_mine, proj_parts, proj_sum, proj_z, proj_y,
+    line_ready, own_sem, in_sem, proj_sem, w_send, w_recv, ex_send, ex_recv,
 ):
     t = lax.axis_index("table")
     f = lax.axis_index("fsdp")
     z, xx, c = f // 8, (f // 2) % 4, f % 2
+    ty, tz = t // 4, t % 4
 
     def fs(dz, dx, dc):
         return ((z + dz) % 3) * 8 + ((xx + dx) % 4) * 2 + (c + dc) % 2
@@ -140,8 +141,7 @@
         def __init__(self, axis, src, dst, index):
             me, self.n = (t, NT) if axis == "table" else (f, NFS)
 
-            def copy(s):
-                to = (me + s) % self.n
+            def copy_to(to):
                 return pltpu.make_async_remote_copy(
                     src_ref=src.at[to] if len(src.shape) == len(dst.shape) else src,
                     dst_ref=dst.at[me],
@@ -151,7 +151,8 @@
                     device_id_type=MESH,
                 )
 
-            self.copy = copy
+            self.copy_to = copy_to
+            self.copy = lambda s: copy_to((me + s) % self.n)
             every = dst.at[pl.ds(0, self.n - 1)]
             self.every = lambda: pltpu.make_async_remote_copy(
                 src_ref=every,
@@ -181,7 +182,32 @@
     row_out = Exchange("table", back, rec_ref, 3)
     all_out = Exchange("table", mine, whole_ref, 4)
     to_fsdp = Exchange("fsdp", blocks, parts, 5)
-    proj_bcast = Exchange("table", proj_sum, proj_all, 6)
+
+
+    def along(src, dst, at, n, to, index):
+        def copy(s):
+            return pltpu.make_async_remote_copy(
+                src_ref=src,
+                dst_ref=dst.at[at],
+                send_sem=proj_sem.at[index],
+                recv_sem=proj_sem.at[index + 1],
+                device_id={"table": to(s)},
+                device_id_type=MESH,
+            )
+
+        every = dst.at[pl.ds(0, n - 1)]
+        both = pltpu.make_async_remote_copy(
+            src_ref=every,
+            dst_ref=every,
+            send_sem=proj_sem.at[index],
+            recv_sem=proj_sem.at[index + 1],
+            device_id={"table": t},
+            device_id_type=MESH,
+        )
+        return (lambda: each(n, lambda s: copy(s).start())), both
+
+    z_start, z_every = along(proj_sum, proj_z, tz, 4, lambda s: ty * 4 + (tz + s) % 4, 2)
+    y_start, y_every = along(proj_y, proj_all, ty, 8, lambda s: ((ty + s) % 8) * 4 + tz, 4)
 
     def local(src, dst, index):
         return pltpu.make_async_copy(src, dst, in_sem.at[index])
@@ -194,8 +220,10 @@
 
     greet("fsdp", near[0])
     greet("fsdp", near[1])
-    for low, high in ((12, 21), (6, 12), (21, 27), (1, 6), (27, NT)):
-        each(high, lambda s: greet("table", (t + s) % NT), low)
+    for dy in (4, 3, 5, 2, 6, 1, 7):
+        greet("table", ((ty + dy) % 8) * 4 + tz)
+    for dz in (2, 3, 1):
+        greet("table", ty * 4 + (tz + dz) % 4)
     for other in near[2:]:
         greet("fsdp", other)
 
@@ -215,7 +243,11 @@
     inputs[1].wait()
     pack[:, :, 0:D] = lk_ref[:, 0]
     pack[:, :, D : 2 * D] = lk_ref[:, 1]
-    pl.semaphore_wait(barrier, NT - 1 + len(near))
+    pl.semaphore_wait(barrier, 10 + len(near))
+    for dz in (2, 3, 1):
+        pl.semaphore_signal(
+            line_ready, inc=1, device_id={"table": ty * 4 + (tz + dz) % 4}, device_id_type=MESH
+        )
 
     def piece(src, shard, part, index, to):
         at = pl.ds(part * HALF_ROWS, HALF_ROWS)
@@ -261,7 +293,10 @@
         send(padded, f, part, 4 + part, right)
         send(padded, f, part, 10 + part, left)
         send(padded, f, part, 22 + part, sibling)
-    row_in.start()
+    started.append(row_in)
+    for dz in range(1, 4):
+        row_in.copy_to(ty * 4 + (tz + dz) % 4).start()
+    each(8, lambda s: row_in.copy_to(((ty + s) % 8) * 4 + tz).start())
     all_ref[pl.ds(f, 1)] = padded[...][None]
     arr[pl.ds(t, 1)] = pack[pl.ds(t, 1)]
 
@@ -272,6 +307,10 @@
     here = jnp.where(lane < NLC, lane + NFM, 2 * ((lane - NLC) % 8) + (lane - NLC) // 8)
     order[...] = one_hot(here == iota((256, 256), 0))
     upstream[...] = nn(cot_ref[...], order[...])
+
+    pl.semaphore_wait(line_ready, 3)
+    for dz in range(1, 4):
+        each(8, lambda s: row_in.copy_to(((ty + s) % 8) * 4 + (tz + dz) % 4).start())
 
     def from_z(part):
         for index, dz in ((0, 2), (2, 1)):
@@ -524,7 +563,6 @@
     blocks[...] = nn(block_place[...], sums).astype(bf16).reshape(NFS, SLOTS, 128)
 
     to_fsdp.start()
-    row_out.start()
 
     @pl.when(f == PROJ_F)
     def _():
@@ -539,8 +577,17 @@
         ).wait_recv()
         proj_parts[pl.ds(f, 1)] = proj_mine[...][None]
         proj_sum[...] = jnp.sum(proj_parts[...].astype(f32), axis=0).astype(bf16)
-        each(NT, lambda s: proj_bcast.copy(s).start())
-        proj_all[pl.ds(t, 1)] = proj_sum[...][None]
+        z_start()
+        proj_z[pl.ds(tz, 1)] = proj_sum[...][None]
+
+    row_out.start()
+
+    @pl.when(f == PROJ_F)
+    def _():
+        z_every.wait_recv()
+        proj_y[...] = jnp.sum(proj_z[...].astype(f32), axis=0).astype(bf16)
+        y_start()
+        proj_all[pl.ds(ty, 1)] = proj_y[...][None]
 
     parts[pl.ds(f, 1)] = blocks[pl.ds(f, 1)]
     to_fsdp.wait()
@@ -553,8 +600,9 @@
 
     @pl.when(f == PROJ_F)
     def _():
-        proj_bcast.wait()
-        proj_bcast.wait_send()
+        y_every.wait_recv()
+        z_every.wait_send()
+        y_every.wait_send()
 
     @pl.when(f != PROJ_F)
     def _():
@@ -593,7 +641,7 @@
             shape(bf16, 2 * D, 256),
             shape(bf16, NT, 16, 2 * D),
             shape(bf16, NT, SLOTS, 128),
-            shape(bf16, NT, 32, 128),
+            shape(bf16, 8, 32, 128),
         ),
         in_specs=[IN_HBM] * 5,
         out_specs=(IN_HBM, VMEM, VMEM, VMEM),
@@ -632,13 +680,16 @@
             pltpu.VMEM((32, 128), bf16),
             pltpu.VMEM((NFS, 32, 128), bf16),
             pltpu.VMEM((32, 128), bf16),
+            pltpu.VMEM((4, 32, 128), bf16),
+            pltpu.VMEM((32, 128), bf16),
+            pltpu.SemaphoreType.REGULAR,
             pltpu.SemaphoreType.DMA((2,)),
             pltpu.SemaphoreType.DMA((6,)),
-            pltpu.SemaphoreType.DMA((2,)),
+            pltpu.SemaphoreType.DMA((6,)),
             pltpu.SemaphoreType.DMA((46,)),
             pltpu.SemaphoreType.DMA((46,)),
-            pltpu.SemaphoreType.DMA((7,)),
-            pltpu.SemaphoreType.DMA((7,)),
+            pltpu.SemaphoreType.DMA((6,)),
+            pltpu.SemaphoreType.DMA((6,)),
         ],
         compiler_params=pltpu.CompilerParams(collective_id=0, has_side_effects=True, vmem_limit_bytes=LIMIT),
     )(*[pltpu.with_memory_space_constraint(v, pltpu.HBM) for v in (looked, shard, as_row, cotangent, jnp.asarray(TO_BLOCK))])

time: 74.1 us -> 71.8 us (0.969)
  the two profiles are of different devices: /device:TPU:2 before, /device:TPU:6 now
where the time goes in v5:
time: 71.8 us; the launch traced here: 71.4 us
  Pallas kernels  70.7 us (98%)
    pallas_call x1, Pallas kernels, whole(): pl.pallas_call(whole_kernel, out_shape=(shape(bf16, 2 * D, 256), shape(bf...  69.5 us

profile of v5, /device:TPU:6, one launch (start us, length us, event | category | flops | bytes accessed | tf_op | source)
XLA Modules:
  0.0 71.4 jit_solution(13982004164905454319)
XLA Ops:
  0.6 0.0 copy-start
  0.6 69.5 %shard_map.85 = (bf16[384,256]{1,0:T(8,128)(2,1)S(1)}, bf16[32,16,384]{2,1,0:T(8,128)(2,1)S(1)}, bf16[32,16,128]{2,1,0:T(8,128)(2,1)S(1)}, bf16[8,32,128]{2,1,0:T(8,128)(2,1)S(1)}) custom-call(bf16[32,2,16,192]{3,2,1,0:T(8,128)(2,1)} %bitcast.11, bf16[340,128]{1,0:T(8,128)(2,1)} %bitcast.13, s32[1,512]{1,0:T(1,128)} %bitcast.14, bf16[384,256]{1,0:T(8,128)(2,1)} %bitcast.12, ...), custom_call_target="tpu_custom_call" | custom-call | tf_op jit(solution)/shard_map/pallas_call | solution.py:638
  70.1 0.0 copy-done
  70.2 1.2 %shard_map.86 = (bf16[384,256]{1,0:T(8,128)(2,1)}, bf16[32,2,16,192]{3,2,1,0:T(8,128)(2,1)}, f32[340,128]{1,0:T(8,128)}) custom-call(bf16[384,256]{1,0:T(8,128)(2,1)S(1)} %get-tuple-element.10.out_ref, bf16[32,16,384]{2,1,0:T(8,128)(2,1)S(1)} %get-tuple-element.11.rec_ref, bf16[32,16,128]{2,1,0:T(8,128)(2,1)S(1)} %get-tuple-element.12.whole_ref, ...), custom_call_target="tpu_custom_call" | custom-call | tf_op jit(solution)/shard_map/pallas_call | solution.py:699
Async XLA Ops:
  0.6 69.5 %copy-start = (s32[24,512]{1,0:T(8,128)S(1)}, s32[24,512]{1,0:T(8,128)}, u32[]{:S(2)}) copy-start(s32[24,512]{1,0:T(8,128)} %constant.5.clone.row_ref) | copy-start | bytes 147460

commit v6 on v5

--- a/solution.py
+++ b/solution.py
@@ -151,6 +151,7 @@
                     device_id_type=MESH,
                 )
 
+            self.order = ((12, 21), (6, 12), (21, 27), (1, 6), (27, NT)) if axis == "table" else ((8, NFS), (1, 8))
             self.copy_to = copy_to
             self.copy = lambda s: copy_to((me + s) % self.n)
             every = dst.at[pl.ds(0, self.n - 1)]
@@ -164,7 +165,8 @@
             )
 
         def start(self):
-            each(self.n, lambda s: self.copy(s).start())
+            for low, high in self.order:
+                each(high, lambda s: self.copy(s).start(), low)
             started.append(self)
 
         def wait(self):

time: 71.8 us -> 70.9 us (0.987)
  Pallas kernels: 70.7 us -> 69.8 us
    pallas_call x1, Pallas kernels: 69.5 us -> 68.6 us  [whole(): pl.pallas_call(whole_kernel, out_shape=(shape(bf16, 2 * D, 256), shape(bf...]
where the time goes in v6:
time: 70.9 us; the launch traced here: 70.4 us
  Pallas kernels  69.8 us (98%)
    pallas_call x1, Pallas kernels, whole(): pl.pallas_call(whole_kernel, out_shape=(shape(bf16, 2 * D, 256), shape(bf...  68.6 us

profile of v6, /device:TPU:6, one launch (start us, length us, event | category | flops | bytes accessed | tf_op | source)
XLA Modules:
  0.0 70.4 jit_solution(12565913707996406282)
XLA Ops:
  0.6 0.0 copy-start
  0.6 68.6 %shard_map.85 = (bf16[384,256]{1,0:T(8,128)(2,1)S(1)}, bf16[32,16,384]{2,1,0:T(8,128)(2,1)S(1)}, bf16[32,16,128]{2,1,0:T(8,128)(2,1)S(1)}, bf16[8,32,128]{2,1,0:T(8,128)(2,1)S(1)}) custom-call(bf16[32,2,16,192]{3,2,1,0:T(8,128)(2,1)} %bitcast.11, bf16[340,128]{1,0:T(8,128)(2,1)} %bitcast.13, s32[1,512]{1,0:T(1,128)} %bitcast.14, bf16[384,256]{1,0:T(8,128)(2,1)} %bitcast.12, ...), custom_call_target="tpu_custom_call" | custom-call | tf_op jit(solution)/shard_map/pallas_call | solution.py:640
  69.2 0.0 copy-done
  69.2 1.2 %shard_map.86 = (bf16[384,256]{1,0:T(8,128)(2,1)}, bf16[32,2,16,192]{3,2,1,0:T(8,128)(2,1)}, f32[340,128]{1,0:T(8,128)}) custom-call(bf16[384,256]{1,0:T(8,128)(2,1)S(1)} %get-tuple-element.10.out_ref, bf16[32,16,384]{2,1,0:T(8,128)(2,1)S(1)} %get-tuple-element.11.rec_ref, bf16[32,16,128]{2,1,0:T(8,128)(2,1)S(1)} %get-tuple-element.12.whole_ref, ...), custom_call_target="tpu_custom_call" | custom-call | tf_op jit(solution)/shard_map/pallas_call | solution.py:701
Async XLA Ops:
  0.6 68.6 %copy-start = (s32[24,512]{1,0:T(8,128)S(1)}, s32[24,512]{1,0:T(8,128)}, u32[]{:S(2)}) copy-start(s32[24,512]{1,0:T(8,128)} %constant.5.clone.row_ref) | copy-start | bytes 147460
